TPU v7x, 32 devices: a whole 2x2x4 slice. The times are simulated.
32 devices in a mesh: pencil: 8 (over z, y), depth: 4 (over x, core).
Axes of the slice: x: 2, y: 2, z: 4, core: 2. Of those that a mesh axis runs over, the one named last changes fastest.
Arguments:
- currents: float32 [2, 24576], P(None, ('pencil', 'depth')), may hold values from -6 to 6
- stencil_cells: int32 [2, 24576], P(None, ('pencil', 'depth')), may hold values from 0 to 2044, as said below
- stencil_weights: float32 [16, 24576], P(None, ('pencil', 'depth')), may hold values from -3 to 3
- soil: float32 [2, 2], replicated, may hold values from 0.3 to 2
- near_pairs: int32 [3, 384], P(None, ('pencil', 'depth')), may hold values from 0 to 17, as said below
- corrections: float32 [384, 2, 128, 128], P(('pencil', 'depth')), may hold values from -0.5 to 0.5
Outputs:
- potentials: float32 [2, 24576], P(None, ('pencil', 'depth'))
Inputs may be any that keep to these rules, and one draw needn't show every extreme that they name: `stencil_cells`: A segment's 16 cells form a 4 x 4 patch in one layer of its device's block: row 0 gives layer * 256 + r with r <= 252, row 1 the first column, at most 2044. `near_pairs`: row 0 holds target blocks below 6; row 1 holds source slots below 18, never naming a device beyond either end of the pencil axis; row 2 holds live flags 0 or 1, the live slots of a device come first, every device has at least one live slot, and some device has all 12 live.
All inputs are finite; a program needn't handle non-finite values.
Results may differ from a plain program's by a relative error of at most 0.00005.
Values sent between devices are 32-bit elements; how exact they have to be, the bound alone decides.
No kernel may reach another device: no remote copies, remote signals or barrier semaphores. Data moves between devices by JAX's collectives and lax.ppermute only.
A program may use at most 192 MiB of HBM per device.

v0:
```python
import math

import jax
import jax.numpy as jnp
from jax import lax
from jax.sharding import PartitionSpec as P

GX = 2048
GY = 2048
ZL = 8


highest = lax.Precision.HIGHEST
layer_step = 1.0
screening = 0.05


def with_halo(cells, sides, width):
    for axis, dim in sides:
        count = lax.axis_size(axis)
        ends = count - 1
        head = lax.slice_in_dim(cells, 0, width, axis=dim)
        tail = lax.slice_in_dim(cells, cells.shape[dim] - width, cells.shape[dim], axis=dim)
        cells = jnp.concatenate(
            [
                lax.ppermute(tail, axis, [(i, (i + 1) % count) for i in range(ends)]),
                cells,
                lax.ppermute(head, axis, [((i + 1) % count, i) for i in range(ends)]),
            ],
            axis=dim,
        )
    return cells


def phase_table(row_count, col_count, modulus, sign):
    first_index = lax.broadcasted_iota(jnp.int32, (row_count, col_count), 0)
    second_index = lax.broadcasted_iota(jnp.int32, (row_count, col_count), 1)
    phase = (first_index * second_index % modulus).astype(jnp.float32) * (2.0 * math.pi / modulus)
    return (jnp.cos(phase), sign * jnp.sin(phase))


def product(form, left, right):
    return jnp.einsum(form, left, right, precision=highest)


def transform_last(pair, sign):
    full_shape = pair.shape
    length = full_shape[-1]
    outer = 1 << (length.bit_length() - 1) // 2
    inner = length // outer
    split_pair = pair.reshape(2, -1, outer, inner)
    real_part, imag_part = (split_pair[0], split_pair[1])
    first_re, first_im = phase_table(outer, outer, outer, sign)
    section_re = product("bpq,pk->bkq", real_part, first_re) - product(
        "bpq,pk->bkq", imag_part, first_im
    )
    section_im = product("bpq,pk->bkq", real_part, first_im) + product(
        "bpq,pk->bkq", imag_part, first_re
    )
    twist_re, twist_im = phase_table(outer, inner, length, sign)
    turned_re = section_re * twist_re - section_im * twist_im
    turned_im = section_re * twist_im + section_im * twist_re
    second_re, second_im = phase_table(inner, inner, inner, sign)
    result_re = product("bkq,qm->bmk", turned_re, second_re) - product(
        "bkq,qm->bmk", turned_im, second_im
    )
    result_im = product("bkq,qm->bmk", turned_re, second_im) + product(
        "bkq,qm->bmk", turned_im, second_re
    )
    return jnp.stack([result_re, result_im]).reshape(full_shape)


def signed_freq(index, length):
    return (
        jnp.where(index < (length - 1) // 2 + 1, index, index - length).astype(jnp.float32) / length
    )


def wavenumbers(first_column, column_count):
    column_index = first_column + jnp.arange(column_count, dtype=jnp.int32)
    freq_y = signed_freq(column_index, GY)
    freq_x = signed_freq(jnp.arange(GX, dtype=jnp.int32), GX)
    return 2.0 * math.pi * jnp.sqrt(freq_y[:, None] ** 2 + freq_x[None, :] ** 2)


def mix_layers(spectrum, kappa, source_layers, soil):
    upper_re, lower_re = (soil[0, 0], soil[0, 1])
    upper_im, lower_im = (soil[1, 0], soil[1, 1])
    denom_re = upper_re + lower_re
    denom_im = upper_im + lower_im
    numer_re = lower_re - upper_re
    numer_im = lower_im - upper_im
    magnitude = denom_re * denom_re + denom_im * denom_im
    refl_re = (numer_re * denom_re + numer_im * denom_im) / magnitude
    refl_im = (numer_im * denom_re - numer_re * denom_im) / magnitude
    is_upper = source_layers < ZL // 2
    rho_re = jnp.where(is_upper, upper_re, lower_re)[:, None, None]
    rho_im = jnp.where(is_upper, upper_im, lower_im)[:, None, None]
    depth_source = source_layers.astype(jnp.float32)[:, None, None]
    base = 1.0 / (GX * GY) / (kappa + screening)
    spec_re, spec_im = (spectrum[0], spectrum[1])
    mixed_re = []
    mixed_im = []
    for layer_out in range(ZL):
        direct = jnp.exp(-kappa * jnp.abs(layer_out - depth_source) * layer_step)
        image = jnp.exp(-kappa * (layer_out + depth_source + 1.0) * layer_step)
        blend_re = direct + refl_re * image
        blend_im = refl_im * image
        green_re = (rho_re * blend_re - rho_im * blend_im) * base
        green_im = (rho_re * blend_im + rho_im * blend_re) * base
        mixed_re.append(jnp.sum(green_re * spec_re - green_im * spec_im, axis=0))
        mixed_im.append(jnp.sum(green_re * spec_im + green_im * spec_re, axis=0))
    return jnp.stack([jnp.stack(mixed_re), jnp.stack(mixed_im)])


def to_pencils(spectrum, pencil_count):
    layer_count = spectrum.shape[1]
    turned = jnp.swapaxes(spectrum, 2, 3)
    return turned.reshape(2, layer_count, pencil_count, -1)


def from_pencils(received, row_count):
    layer_count, pencil_count = (received.shape[1], received.shape[2])
    opened = received.reshape(2, layer_count, pencil_count, -1, row_count)
    opened = jnp.transpose(opened, (0, 1, 3, 2, 4))
    return opened.reshape(2, layer_count, -1, pencil_count * row_count)


def to_rows(field, pencil_count):
    layer_count, column_count = (field.shape[1], field.shape[2])
    opened = field.reshape(2, layer_count, column_count, pencil_count, -1)
    opened = jnp.transpose(opened, (0, 1, 3, 2, 4))
    return opened.reshape(2, layer_count, pencil_count, -1)


def from_rows(received, row_count):
    layer_count = received.shape[1]
    opened = received.reshape(2, layer_count, -1, row_count)
    return jnp.swapaxes(opened, 2, 3)


def row_factor(first_rows, weights, total_rows):
    seg_count = first_rows.shape[0]
    row_index = lax.broadcasted_iota(jnp.int32, (total_rows, seg_count), 0)
    stencil = weights.reshape(4, 4, seg_count)
    factor = jnp.zeros((4, total_rows, seg_count), jnp.float32)
    for offset in range(4):
        select = (row_index == (first_rows + offset)[None, :]).astype(jnp.float32)
        factor = factor + stencil[offset][:, None, :] * select[None, :, :]
    return factor


def shards(currents, stencil_cells, stencil_weights, soil, near_pairs, corrections):
    pencil_count = lax.axis_size("pencil")
    depth_count = lax.axis_size("depth")
    pencil_index = lax.axis_index("pencil")
    depth_index = lax.axis_index("depth")
    seg_count = currents.shape[1]
    layer_count = ZL // depth_count
    row_count = GX // pencil_count
    column_count = GY // pencil_count
    quarter = column_count // depth_count
    total_rows = layer_count * row_count
    weighted_rows = row_factor(stencil_cells[0], stencil_weights, total_rows)
    column_index = lax.broadcasted_iota(jnp.int32, (seg_count, GY), 1)
    column_select = (column_index == stencil_cells[1][:, None]).astype(jnp.float32)
    spread_left = (weighted_rows[None] * currents[:, None, None, :]).reshape(
        2 * 4 * total_rows, seg_count
    )
    spread = jnp.dot(spread_left, column_select, precision=highest).reshape(2, 4, total_rows, GY)
    grid = jnp.zeros((2, total_rows, GY), jnp.float32)
    for offset in range(4):
        moved = jnp.pad(spread[:, offset], ((0, 0), (0, 0), (offset, 0)))[:, :, :GY]
        grid = grid + moved
    grid = grid.reshape(2, layer_count, row_count, GY)
    row_spectrum = transform_last(grid, -1.0)
    all_layers = jnp.arange(ZL, dtype=jnp.int32)
    outgoing = to_pencils(row_spectrum, pencil_count)
    arrived = lax.all_to_all(outgoing, "pencil", split_axis=2, concat_axis=2, tiled=True)
    spectrum = transform_last(from_pencils(arrived, row_count), -1.0)
    grouped = lax.all_to_all(spectrum, "depth", split_axis=2, concat_axis=1, tiled=True)
    kappa = wavenumbers(pencil_index * column_count + depth_index * quarter, quarter)
    mixed = mix_layers(grouped, kappa, all_layers, soil)
    ungrouped = lax.all_to_all(mixed, "depth", split_axis=1, concat_axis=2, tiled=True)
    leaving = to_rows(transform_last(ungrouped, 1.0), pencil_count)
    returned = lax.all_to_all(leaving, "pencil", split_axis=2, concat_axis=2, tiled=True)
    potential = from_rows(returned, row_count)
    grid_field = transform_last(potential, 1.0).reshape(2, total_rows, GY)
    shifted = []
    for offset in range(4):
        shifted.append(
            jnp.pad(grid_field, ((0, 0), (0, 0), (0, offset)))[:, :, offset : offset + GY]
        )
    stacked = jnp.stack(shifted, axis=1).reshape(2 * 4 * total_rows, GY)
    sampled = lax.dot_general(stacked, column_select, (((1,), (1,)), ((), ())), precision=highest)
    sampled = sampled.reshape(2, 4, total_rows, seg_count)
    far = jnp.sum(sampled * weighted_rows[None], axis=(1, 2))
    block_size = corrections.shape[2]
    block_count = seg_count // block_size
    blocks = currents.reshape(2, block_count, block_size)
    beside_all = with_halo(blocks, (("pencil", 1),), block_count)
    targets, sources, live = (near_pairs[0], near_pairs[1], near_pairs[2])
    source_select = (
        sources[:, None] == jnp.arange(3 * block_count, dtype=jnp.int32)[None, :]
    ).astype(jnp.float32)
    picked = product("pk,ckj->cpj", source_select, beside_all)
    piece_re = product("pij,pj->pi", corrections[:, 0], picked[0]) - product(
        "pij,pj->pi", corrections[:, 1], picked[1]
    )
    piece_im = product("pij,pj->pi", corrections[:, 0], picked[1]) + product(
        "pij,pj->pi", corrections[:, 1], picked[0]
    )
    owner = (targets[:, None] == jnp.arange(block_count, dtype=jnp.int32)[None, :]).astype(
        jnp.float32
    ) * live.astype(jnp.float32)[:, None]
    near = jnp.stack([product("pt,pi->ti", owner, piece_re), product("pt,pi->ti", owner, piece_im)])
    return far + near.reshape(2, seg_count)


def solution(mesh):
    return jax.shard_map(
        shards,
        mesh=mesh,
        in_specs=(
            P(None, ("pencil", "depth")),
            P(None, ("pencil", "depth")),
            P(None, ("pencil", "depth")),
            P(),
            P(None, ("pencil", "depth")),
            P(("pencil", "depth"), None, None, None),
        ),
        out_specs=P(None, ("pencil", "depth")),
        check_vma=False,
    )
```

profile of v0, /device:TPU:1, one launch (start us, length us, event | category | flops | bytes accessed | tf_op | source)
XLA Modules:
  0.0 1395.5 jit_solution(16671343553048135616)
XLA Ops:
  7.3 44.1 %fusion.10 = f32[2,4,512,2048]{3,2,1,0:T(8,128)} fusion(f32[2,768]{1,0:T(2,128)S(1)} %copy-done.24, f32[4,512,768]{2,1,0:T(8,128)S(1)} %multiply_add_fusion, pred[768,2048,1,1]{1,0,3,2:T(32,128)(4,1)S(1)} %fusion.461), kind=kOutput, calls=%fused_computation.11 | convolution fusion | flops 77312557056 | bytes 41424896 | tf_op jit(solution)/shard_map/dot_general | solution.py:170
  51.5 17.6 %slice_bitcast_fusion = (f32[2,512,2048]{2,1,0:T(8,128)}, f32[2,512,2048]{2,1,0:T(8,128)}, f32[2,512,2048]{2,1,0:T(8,128)}) fusion(f32[2,4,512,2048]{3,2,1,0:T(8,128)} %fusion.10), kind=kLoop, calls=%fused_computation.25 | loop fusion | bytes 50331648 | tf_op jit(solution)/shard_map/squeeze | solution.py:173
  69.1 23.5 %fusion.14 = f32[2,512,2048]{2,1,0:T(8,128)S(1)} fusion(f32[2,512,2048]{2,1,0:T(8,128)} %get-tuple-element.35, f32[2,512,2048]{2,1,0:T(8,128)} %get-tuple-element.36, f32[2,512,2048]{2,1,0:T(8,128)} %get-tuple-element.34, f32[2,4,512,2048]{3,2,1,0:T(8,128)} %fusion.10), kind=kLoop, calls=%fused_computation.21 | loop fusion | flops 6291456 | bytes 41943040 | tf_op jit(solution)/shard_map/add | solution.py:174
  102.2 10.2 fusion.81
  125.1 10.0 fusion.93
  173.0 9.4 add_bitcast_fusion.6
  209.9 14.8 %copy.231 = f32[2,2,8,65536]{3,1,0,2:T(2,128)S(1)} copy(f32[2,2,8,65536]{3,2,1,0:T(8,128)} %reshape.943) | data formatting | bytes 16777216 | tf_op jit(solution)/shard_map/reshape | solution.py:119
  224.7 188.5 %all_to_all.40 = f32[2,2,8,65536]{3,1,0,2:T(2,128)} all-to-all(f32[2,2,8,65536]{3,1,0,2:T(2,128)S(1)} %copy.231), channel_id=1, replica_groups=mesh['pencil'=8,'depth'=4] {'pencil'}, dimensions={2} | all-to-all | bytes 16777216 | tf_op jit(solution)/shard_map/all_to_all | solution.py:179
  413.3 15.1 %reshape.944 = f32[2,2,8,256,256]{4,3,1,0,2:T(8,128)} reshape(f32[2,2,8,65536]{3,1,0,2:T(2,128)} %all_to_all.40) | data formatting | bytes 16777216 | tf_op jit(solution)/shard_map/reshape | solution.py:124
  428.3 13.1 copy.232
  441.5 10.3 fusion.425
  458.2 10.1 fusion.65
  482.1 9.9 fusion.103
  529.9 9.4 add_bitcast_fusion.4
  558.0 17.3 %copy.243 = f32[2,2,256,2048]{3,1,0,2:T(2,128)} copy(f32[2,2,256,2048]{2,1,3,0:T(2,128)} %pad_maximum_fusion) | data formatting | bytes 16777216 | tf_op jit(solution)/shard_map/stack | solution.py:70
  591.9 83.7 %all-to-all-done.1 = f32[2,2,256,2048]{3,1,0,2:T(2,128)} async-done(((f32[2,2,256,2048]{3,1,0,2:T(2,128)}), f32[2,2,256,2048]{3,1,0,2:T(2,128)}, u32[]{:S(2)}, u32[]{:S(2)}) %all-to-all-start.1) | async-done | bytes 8388640 | tf_op jit(solution)/shard_map/all_to_all | solution.py:181
  683.8 16.2 %subtract_reduce_fusion.1 = (f32[64,2048]{1,0:T(8,128)S(1)}, f32[64,2048]{1,0:T(8,128)S(1)}, f32[64,2048]{1,0:T(8,128)S(1)}, f32[64,2048]{1,0:T(8,128)S(1)}, f32...) fusion(f32[4,2]{0,1:T(2,128)S(1)} %get-tuple-element.89, ...), kind=kLoop, calls=%fused_computation.61 | loop fusion | flops 87031808 | bytes 13631816 | tf_op jit(solution)/shard_map/reduce_sum | solution.py:111
  700.1 17.5 %subtract_reduce_fusion.2 = (f32[64,2048]{1,0:T(8,128)S(1)}, f32[64,2048]{1,0:T(8,128)S(1)}, f32[64,2048]{1,0:T(8,128)S(1)}, f32[64,2048]{1,0:T(8,128)S(1)}, f32...) fusion(f32[4,2]{0,1:T(2,128)S(1)} %get-tuple-element.100, ...), kind=kLoop, calls=%fused_computation.67 | loop fusion | flops 87031808 | bytes 13631816 | tf_op jit(solution)/shard_map/reduce_sum | solution.py:111
  728.9 92.2 %all-to-all-done.2 = f32[2,8,64,2048]{3,2,0,1:T(8,128)} async-done(((f32[2,8,64,2048]{3,2,0,1:T(8,128)}), f32[2,8,64,2048]{3,2,0,1:T(8,128)}, u32[]{:S(2)}, u32[]{:S(2)}) %all-to-all-start.2) | async-done | bytes 8388640 | tf_op jit(solution)/shard_map/all_to_all | solution.py:184
  919.9 9.4 add_bitcast_fusion.2
  947.9 13.1 copy.288
  961.1 14.2 %reshape.962 = f32[2,2,8,65536]{3,1,0,2:T(2,128)} reshape(f32[2,2,8,256,256]{4,3,1,0,2:T(8,128)} %copy.288) | data formatting | bytes 16777216 | tf_op jit(solution)/shard_map/reshape | solution.py:133
  986.3 61.3 %collective-permute-done = f32[2,6,128]{2,1,0:T(8,128)S(1)} collective-permute-done((f32[2,6,128]{2,1,0:T(8,128)S(1)}, f32[2,6,128]{2,1,0:T(8,128)S(1)}, u32[]{:S(2)}, u32[]{:S(2)}) %collective-permute-start) | collective-permute-done | bytes 6176 | tf_op jit(solution)/shard_map/ppermute | solution.py:26
  1053.7 108.9 %all-to-all-done.3 = f32[2,2,8,65536]{3,1,0,2:T(2,128)} async-done(((f32[2,2,8,65536]{3,1,0,2:T(2,128)}), f32[2,2,8,65536]{3,1,0,2:T(2,128)}, u32[]{:S(2)}, u32[]{:S(2)}) %all-to-all-start.3) | async-done | bytes 8388640 | tf_op jit(solution)/shard_map/all_to_all | solution.py:186
  1162.6 11.5 copy.260
  1187.5 12.2 copy.263
  1206.1 10.1 fusion.41
  1223.6 12.2 copy.261
  1242.6 10.0 fusion.117
  1290.1 9.4 add_bitcast_fusion
  1317.2 19.9 %fusion.15 = (f32[2,1,512,2048]{3,2,1,0:T(8,128)}, f32[2,1,512,2048]{3,2,1,0:T(8,128)}, f32[2,1,512,2048]{3,2,1,0:T(8,128)}) fusion(f32[2,512,2048]{2,1,0:T(8,128)} %pad_maximum_fusion.2), kind=kLoop, calls=%fused_computation.22 | loop fusion | bytes 33554432 | tf_op jit(solution)/shard_map/stack | solution.py:194
  1348.0 46.8 %multiply_reduce_fusion = f32[2,768]{1,0:T(2,128)S(1)} fusion(f32[4,512,768]{2,1,0:T(8,128)} %copy-done.18, f32[2,1,512,2048]{3,2,1,0:T(8,128)} %get-tuple-element.54, f32[2,1,512,2048]{3,2,1,0:T(8,128)} %get-tuple-element.55, f32[2,1,512,2048]{3,2,1,0:T(8,128)} %get-tuple-element.53, f32[1,1,512,2048]{3,2,1,0:T(8,128)} %copy.274, ...), kind=kOutput, calls=%fused_computation.10 | convolution fusion | flops 77349257216 | bytes 41424896 | tf_op jit(solution)/shard_map/dot_general | solution.py:195
  (177 shorter events, 437.6 us)
Async XLA Ops:
  3.1 4.2 copy-start.24
  4.6 2.7 copy-start.18
  102.2 10.2 copy-start.9
  125.1 10.0 copy-start.6
  125.1 10.0 copy-start.12
  142.7 13.6 copy-start.2
  458.2 10.1 copy-start.10
  482.1 10.0 copy-start.7
  482.1 10.0 copy-start.15
  499.5 13.8 copy-start
  575.3 8.0 copy-start.26
  575.3 100.3 %all-to-all-start.1 = ((f32[2,2,256,2048]{3,1,0,2:T(2,128)}), f32[2,2,256,2048]{3,1,0,2:T(2,128)}, u32[]{:S(2)}, u32[]{:S(2)}) async-start(f32[2,2,256,2048]{3,1,0,2:T(2,128)} %copy.243), calls=%async_computation.1 | async-start | bytes 16777216 | tf_op jit(solution)/shard_map/all_to_all | solution.py:181
  591.8 92.0 %copy-start.20 = (f32[64,2048]{1,0:T(8,128)}, f32[64,2048]{1,0:T(8,128)S(1)}, u32[]{:S(2)}) copy-start(f32[64,2048]{1,0:T(8,128)S(1)} %get-tuple-element.70) | copy-start | bytes 1572868
  591.8 92.0 %copy-start.21 = (f32[64,2048]{1,0:T(8,128)}, f32[64,2048]{1,0:T(8,128)S(1)}, u32[]{:S(2)}) copy-start(f32[64,2048]{1,0:T(8,128)S(1)} %get-tuple-element.71) | copy-start | bytes 1572868
  722.0 99.0 %all-to-all-start.2 = ((f32[2,8,64,2048]{3,2,0,1:T(8,128)}), f32[2,8,64,2048]{3,2,0,1:T(8,128)}, u32[]{:S(2)}, u32[]{:S(2)}) async-start(f32[2,8,64,2048]{3,2,0,1:T(8,128)} %pad_maximum_fusion.1), calls=%async_computation.2 | async-start | bytes 16777216 | tf_op jit(solution)/shard_map/all_to_all | solution.py:184
  845.5 8.0 copy-start.8
  853.5 5.3 copy-start.16
  876.9 7.7 copy-start.4
  876.9 7.7 copy-start.13
  889.6 13.6 copy-start.3
  975.3 5.1 copy-start.25
  975.3 10.1 copy-start.23
  975.3 11.0 copy-start.27
  975.3 72.5 %copy-start.19 = (f32[12,2,128,128]{3,2,1,0:T(8,128)S(1)}, f32[12,2,128,128]{3,2,1,0:T(8,128)}, u32[]{:S(2)}) copy-start(f32[12,2,128,128]{3,2,1,0:T(8,128)} %param.11) | copy-start | bytes 4718596
  975.3 187.3 %all-to-all-start.3 = ((f32[2,2,8,65536]{3,1,0,2:T(2,128)}), f32[2,2,8,65536]{3,1,0,2:T(2,128)}, u32[]{:S(2)}, u32[]{:S(2)}) async-start(f32[2,2,8,65536]{3,1,0,2:T(2,128)} %reshape.962), calls=%async_computation.3 | async-start | bytes 16777216 | tf_op jit(solution)/shard_map/all_to_all | solution.py:186
  980.4 67.2 %collective-permute-start = (f32[2,6,128]{2,1,0:T(8,128)S(1)}, f32[2,6,128]{2,1,0:T(8,128)S(1)}, u32[]{:S(2)}, u32[]{:S(2)}) collective-permute-start(f32[2,6,128]{2,1,0:T(8,128)S(1)} %reshape.947), channel_id=1, source_target_pairs={{0,4},{4,8},{8,12},{12,16},{16,20},{20,24},{24,28},{1,5},{5,9},{9,... | collective-permute-start | bytes 18440 | tf_op jit(solution)/shard_map/ppermute | solution.py:26
  983.6 63.9 %collective-permute-start.1 = (f32[2,6,128]{2,1,0:T(8,128)S(1)}, f32[2,6,128]{2,1,0:T(8,128)S(1)}, u32[]{:S(2)}, u32[]{:S(2)}) collective-permute-start(f32[2,6,128]{2,1,0:T(8,128)S(1)} %reshape.947), channel_id=1, source_target_pairs={{4,0},{8,4},{12,8},{16,12},{20,16},{24,20},{28,24},{5,1},{9,5},{13... | collective-permute-start | bytes 18440 | tf_op jit(solution)/shard_map/ppermute | solution.py:28
  1206.1 10.1 copy-start.11
  1216.3 7.3 copy-start.17
  1242.6 10.0 copy-start.5
  1242.6 10.0 copy-start.14
  1260.0 13.6 copy-start.1
  (1 other events, 2.3 us)
where the time goes:
time: 1410 us; the launch traced here: 1400 us
  local copies, waits for them, and re-layouts  386 us (27%)
  waiting for transfers between devices  346 us (25%)
  matrix products  344 us (24%)
  blocking collectives  189 us (13%)
  other arithmetic  99.7 us (7%)
  starting transfers between devices  24.6 us (2%)
    dot_general x39, matrix products, product(): return jnp.einsum(form, left, right, precision=highest)  253 us
    all_to_all x1, blocking collectives, shards(): lax.all_to_all(outgoing, 'pencil', split_axis=2, concat_axis=2, tiled=True)  189 us
    all_to_all x1, waiting for transfers between devices, shards(): lax.all_to_all(leaving, 'pencil', split_axis=2, concat_axis=2, tiled=True)  109 us
    all_to_all x1, waiting for transfers between devices, shards(): lax.all_to_all(mixed, 'depth', split_axis=1, concat_axis=2, tiled=True)  92.2 us
    all_to_all x1, waiting for transfers between devices, shards(): lax.all_to_all(spectrum, 'depth', split_axis=2, concat_axis=1, tiled=True)  83.7 us
    another operation x11, local copies, waits for them, and re-layouts, transform_last(): return jnp.stack([result_re, result_im]).reshape(full_shape)  75.2 us
    slice x10, local copies, waits for them, and re-layouts, transform_last(): real_part, imag_part = (split_pair[0], split_pair[1])  63.1 us
    ppermute x1, waiting for transfers between devices, with_halo(): lax.ppermute(tail, axis, [(i, (i + 1) % count) for i in range(ends)])  61.3 us
  transfers between devices with their start and end apart: 5, of which 4 were waited for; matrix products, arithmetic and copies ran while one was open for 1% of the time, Pallas kernels for 0%

commit v1 on v0

v1 whole, which is shorter than its diff:
```python
import functools
import math

import jax
import jax.numpy as jnp
import ml_dtypes
import numpy as np
from jax import lax
from jax.experimental import pallas as pl
from jax.experimental.pallas import tpu as pltpu
from jax.sharding import PartitionSpec as P

GX = 2048
GY = 2048
ZL = 8

LANES = 256
RADIX = GX // LANES
FINE = 8
SPAN = 16
COLUMNS = 64
FIELDS = 24
TILE = 16

highest = lax.Precision.HIGHEST
screening = 0.05
f32 = jnp.float32
bf16 = jnp.bfloat16


def product(form, left, right):
    return jnp.einsum(form, left, right, precision=highest)


def halves(value):
    high = value.astype(bf16)
    return high, (value - high.astype(f32)).astype(bf16)


def host_halves(value):
    value = value.astype(np.float32)
    high = value.astype(ml_dtypes.bfloat16)
    return high, (value - high.astype(np.float32)).astype(ml_dtypes.bfloat16)


def column_tables():
    ky = np.arange(GY)[:, None]

    def table(offsets):
        phase = (ky * offsets[None, :] % GY) * (2.0 * math.pi / GY)
        return np.stack([np.cos(phase), -np.sin(phase)], axis=0)

    fine_high, fine_low = host_halves(table(np.arange(SPAN)))
    coarse_high, coarse_low = host_halves(table(FINE * np.arange(GY // FINE)))
    fine = np.concatenate([fine_high, fine_high, fine_low], axis=2)
    coarse = np.concatenate([coarse_high, coarse_low], axis=2)
    return fine, coarse


def transform_tables():
    index = np.arange(LANES)
    phase = (index[:, None] * index[None, :] % LANES) * (2.0 * math.pi / LANES)
    cos, sin = np.cos(phase), np.sin(phase)
    forward = np.block([[cos, -sin], [sin, cos]])
    twist = (np.arange(RADIX)[:, None] * index[None, :]) * (2.0 * math.pi / GX)
    twists = np.stack([np.cos(twist), -np.sin(twist)]).astype(np.float32)
    return np.stack(host_halves(forward)), np.stack(host_halves(forward.T)), twists


def segment_factors(fields, fine_ref, coarse_ref):
    count = fields.shape[1]
    column = fields[19:20].astype(jnp.int32)
    coarse_index = lax.broadcasted_iota(jnp.int32, (GY // FINE, count), 0)
    pick = jnp.where(coarse_index == column // FINE, 1.0, 0.0).astype(bf16)
    coarse = jnp.dot(
        coarse_ref[...], jnp.concatenate([pick, pick], axis=0), preferred_element_type=f32
    )
    fine_index = lax.broadcasted_iota(jnp.int32, (SPAN, count), 0) - column % FINE
    at = [fine_index == offset for offset in range(4)]
    parts = []
    for a in range(4):
        spread = jnp.zeros((SPAN, count), f32)
        for b in range(4):
            spread = jnp.where(at[b], fields[4 * a + b : 4 * a + b + 1], spread)
        high, low = halves(spread)
        parts.append(jnp.concatenate([high, low, high], axis=0))
    fine = jnp.dot(fine_ref[...], jnp.concatenate(parts, axis=1), preferred_element_type=f32)
    fines = [fine[:, a * count : (a + 1) * count] for a in range(4)]
    return coarse, fines


def row_select(fields, total_rows):
    row = fields[18:19].astype(jnp.int32)
    row_index = lax.broadcasted_iota(jnp.int32, (total_rows, fields.shape[1]), 0)
    return jnp.where(row_index == row, 1.0, 0.0).astype(bf16)


def spread_kernel(fields_ref, fine_ref, coarse_ref, out_ref, *, repeats):
    fields = fields_ref[0]
    layers = out_ref.shape[0]
    coarse, fines = segment_factors(fields, fine_ref, coarse_ref)
    current_re, current_im = fields[16:17], fields[17:18]
    phase_re, phase_im = coarse[:COLUMNS], coarse[COLUMNS:]
    wave_re = phase_re * current_re - phase_im * current_im
    wave_im = phase_re * current_im + phase_im * current_re
    parts = []
    for fine in fines:
        fine_re, fine_im = fine[:COLUMNS], fine[COLUMNS:]
        parts.append(halves(wave_re * fine_re - wave_im * fine_im))
        parts.append(halves(wave_re * fine_im + wave_im * fine_re))
    select = row_select(fields, layers * LANES)
    form = (((1,), (1,)), ((), ()))
    spread = sum(
        lax.dot_general(
            jnp.concatenate([part[i] for part in parts], axis=0),
            select,
            form,
            preferred_element_type=f32,
        )
        for i in range(2)
    )
    total = spread[: 2 * COLUMNS]
    for a in range(1, 4):
        total = total + pltpu.roll(spread[2 * COLUMNS * a : 2 * COLUMNS * (a + 1)], a, 1)
    for layer in range(layers):
        piece = total[:, layer * LANES : (layer + 1) * LANES]
        if repeats == 1:
            out_ref[layer] = piece
        else:
            fresh = pl.program_id(2) == 0
            out_ref[layer] = jnp.where(fresh, 0.0, out_ref[layer]) + piece


def sample_kernel(fields_ref, field_ref, fine_ref, coarse_ref, out_ref):
    fields = fields_ref[0]
    layers = field_ref.shape[0]
    total_rows = layers * LANES
    coarse, fines = segment_factors(fields, fine_ref, coarse_ref)
    select = row_select(fields, total_rows)
    field = jnp.concatenate([field_ref[layer] for layer in range(layers)], axis=1)
    parts = [halves(field)]
    for a in range(1, 4):
        parts.append(halves(pltpu.roll(field, total_rows - a, 1)))
    sampled = sum(
        jnp.dot(
            jnp.concatenate([part[i] for part in parts], axis=0),
            select,
            preferred_element_type=f32,
        )
        for i in range(2)
    )
    sum_re, sum_im = 0.0, 0.0
    for a, fine in enumerate(fines):
        fine_re, fine_im = fine[:COLUMNS], fine[COLUMNS:]
        base = 2 * COLUMNS * a
        value_re = sampled[base : base + COLUMNS]
        value_im = sampled[base + COLUMNS : base + 2 * COLUMNS]
        sum_re = sum_re + value_re * fine_re + value_im * fine_im
        sum_im = sum_im + value_im * fine_re - value_re * fine_im
    phase_re, phase_im = coarse[:COLUMNS], coarse[COLUMNS:]
    far_re = jnp.sum(sum_re * phase_re + sum_im * phase_im, axis=0, keepdims=True)
    far_im = jnp.sum(sum_im * phase_re - sum_re * phase_im, axis=0, keepdims=True)
    out_ref[0] = jnp.concatenate([far_re, far_im], axis=0)


def turn(value, step, size, sign):
    real, imag = value
    eighth = step * (8 // size)
    if eighth == 0:
        return value
    if eighth == 2:
        return (-sign * imag, sign * real) if sign > 0 else (imag, -real)
    half = math.sqrt(0.5)
    if eighth == 1:
        if sign > 0:
            return ((real - imag) * half, (real + imag) * half)
        return ((real + imag) * half, (imag - real) * half)
    if sign > 0:
        return ((real + imag) * -half, (real - imag) * half)
    return ((imag - real) * half, (real + imag) * -half)


def butterflies(values, sign):
    size = len(values)
    if size == 1:
        return values
    even = butterflies(values[0::2], sign)
    odd = butterflies(values[1::2], sign)
    low, high = [], []
    for k in range(size // 2):
        moved = turn(odd[k], k, size, sign)
        low.append((even[k][0] + moved[0], even[k][1] + moved[1]))
        high.append((even[k][0] - moved[0], even[k][1] - moved[1]))
    return low + high


def dense(value, matrix_ref):
    high, low = halves(value)
    return (
        jnp.dot(high, matrix_ref[0], preferred_element_type=f32)
        + jnp.dot(low, matrix_ref[0], preferred_element_type=f32)
        + jnp.dot(high, matrix_ref[1], preferred_element_type=f32)
    )


def mix(spec, kappa, keep, soil_ref):
    upper = (soil_ref[0], soil_ref[1])
    lower = (soil_ref[2], soil_ref[3])
    refl_re, refl_im = soil_ref[4], soil_ref[5]
    decay = jnp.exp(-kappa)
    base = jnp.where(keep, 1.0 / (GX * GY) / (kappa + screening), 0.0)
    source = []
    for layer in range(ZL):
        rho_re, rho_im = upper if layer < ZL // 2 else lower
        re, im = spec[layer]
        source.append(((rho_re * re - rho_im * im) * base, (rho_re * im + rho_im * re) * base))
    below = [None] * ZL
    below[ZL - 1] = (jnp.zeros_like(kappa), jnp.zeros_like(kappa))
    for layer in range(ZL - 2, -1, -1):
        below[layer] = tuple(decay * (below[layer + 1][i] + source[layer + 1][i]) for i in range(2))
    surface = tuple(decay * (below[0][i] + source[0][i]) for i in range(2))
    image = (
        refl_re * surface[0] - refl_im * surface[1],
        refl_re * surface[1] + refl_im * surface[0],
    )
    above = source[0]
    mixed = []
    for layer in range(ZL):
        if layer:
            above = tuple(decay * above[i] + source[layer][i] for i in range(2))
            image = tuple(decay * image[i] for i in range(2))
        mixed.append(tuple(above[i] + below[layer][i] + image[i] for i in range(2)))
    return mixed


def mix_kernel(first_ref, soil_ref, spec_ref, forward_ref, inverse_ref, twist_ref, out_ref, *, columns):
    tile = spec_ref.shape[2]
    rows = ZL * tile
    real = spec_ref[:, 0].reshape(rows, GX)
    imag = spec_ref[:, 1].reshape(rows, GX)
    cut = [slice(n * LANES, (n + 1) * LANES) for n in range(RADIX)]
    values = butterflies([(real[:, c], imag[:, c]) for c in cut], -1.0)
    local = pl.program_id(0) * tile + lax.broadcasted_iota(jnp.int32, (tile, LANES), 0)
    keep = local < columns
    ky = first_ref[0] + local
    freq_y = jnp.where(ky < (GY - 1) // 2 + 1, ky, ky - GY).astype(f32) / GY
    inner = lax.broadcasted_iota(jnp.int32, (tile, LANES), 1)
    back = []
    for k in range(RADIX):
        twist_re, twist_im = twist_ref[0, k : k + 1], twist_ref[1, k : k + 1]
        re, im = values[k]
        turned = (re * twist_re - im * twist_im, re * twist_im + im * twist_re) if k else (re, im)
        spectrum = dense(jnp.concatenate(turned, axis=1), forward_ref)
        kx = k + RADIX * inner
        freq_x = jnp.where(kx < (GX - 1) // 2 + 1, kx, kx - GX).astype(f32) / GX
        kappa = 2.0 * math.pi * jnp.sqrt(freq_x * freq_x + freq_y * freq_y)
        spec = [
            (spectrum[s * tile : (s + 1) * tile, :LANES], spectrum[s * tile : (s + 1) * tile, LANES:])
            for s in range(ZL)
        ]
        mixed = mix(spec, kappa, keep, soil_ref)
        stacked = jnp.concatenate([jnp.concatenate(pair, axis=1) for pair in mixed], axis=0)
        field = dense(stacked, inverse_ref)
        re, im = field[:, :LANES], field[:, LANES:]
        turned = (re * twist_re + im * twist_im, im * twist_re - re * twist_im) if k else (re, im)
        back.append(turned)
    values = butterflies(back, 1.0)
    for n in range(RADIX):
        out_ref[:, 0, :, cut[n]] = values[n][0].reshape(ZL, tile, LANES)
        out_ref[:, 1, :, cut[n]] = values[n][1].reshape(ZL, tile, LANES)


def everyone(value, axis):
    count = lax.axis_size(axis)
    copies = jnp.broadcast_to(value[None], (count,) + value.shape)
    return lax.all_to_all(copies, axis, split_axis=0, concat_axis=0, tiled=True)


def near_field(beside, near_pairs, corrections):
    block_size = corrections.shape[2]
    block_count = beside.shape[2] // block_size
    slots = beside.shape[0] * block_count
    blocks = jnp.swapaxes(beside, 0, 1).reshape(2, slots, block_size)
    targets, sources, live = (near_pairs[0], near_pairs[1], near_pairs[2])
    source_select = (sources[:, None] == jnp.arange(slots, dtype=jnp.int32)[None, :]).astype(f32)
    picked = product("pk,ckj->cpj", source_select, blocks)
    piece_re = product("pij,pj->pi", corrections[:, 0], picked[0]) - product(
        "pij,pj->pi", corrections[:, 1], picked[1]
    )
    piece_im = product("pij,pj->pi", corrections[:, 0], picked[1]) + product(
        "pij,pj->pi", corrections[:, 1], picked[0]
    )
    owner = (targets[:, None] == jnp.arange(block_count, dtype=jnp.int32)[None, :]).astype(
        f32
    ) * live.astype(f32)[:, None]
    near = jnp.stack([product("pt,pi->ti", owner, piece_re), product("pt,pi->ti", owner, piece_im)])
    return near.reshape(2, block_count * block_size)


def soil_scalars(soil):
    upper_re, lower_re = (soil[0, 0], soil[0, 1])
    upper_im, lower_im = (soil[1, 0], soil[1, 1])
    denom_re, denom_im = upper_re + lower_re, upper_im + lower_im
    numer_re, numer_im = lower_re - upper_re, lower_im - upper_im
    magnitude = denom_re * denom_re + denom_im * denom_im
    refl_re = (numer_re * denom_re + numer_im * denom_im) / magnitude
    refl_im = (numer_im * denom_re - numer_re * denom_im) / magnitude
    return jnp.stack([upper_re, upper_im, lower_re, lower_im, refl_re, refl_im])


def shards(currents, stencil_cells, stencil_weights, soil, near_pairs, corrections):
    pencils = lax.axis_size("pencil")
    depths = lax.axis_size("depth")
    pencil = lax.axis_index("pencil")
    depth = lax.axis_index("depth")
    segments = currents.shape[1]
    layers = ZL // depths
    rows = GX // pencils
    repeats = LANES // rows
    groups = pencils * depths
    columns = GY // groups
    first = (pencil * depths + depth) * columns

    row = stencil_cells[0] // rows * LANES + pencil % repeats * rows + stencil_cells[0] % rows
    fields = jnp.concatenate(
        [
            stencil_weights,
            currents,
            row[None].astype(f32),
            stencil_cells[1:2].astype(f32),
            jnp.zeros((FIELDS - 20, segments), f32),
        ]
    )
    gathered = everyone(everyone(fields, "pencil"), "depth")

    fine, coarse = column_tables()
    fine = lax.dynamic_slice_in_dim(
        jnp.asarray(np.pad(fine, ((0, 0), (0, COLUMNS), (0, 0)))), first, COLUMNS, axis=1
    ).reshape(2 * COLUMNS, -1)
    coarse = lax.dynamic_slice_in_dim(
        jnp.asarray(np.pad(coarse, ((0, 0), (0, COLUMNS), (0, 0)))), first, COLUMNS, axis=1
    ).reshape(2 * COLUMNS, -1)
    forward, inverse, twists = transform_tables()

    steps = (GX // LANES, depths, repeats)
    fields_spec = pl.BlockSpec(
        (None, 1, FIELDS, segments), lambda p, d, r: (d, p * repeats + r, 0, 0)
    )
    grid_spec = pl.BlockSpec((layers, 2 * COLUMNS, LANES), lambda p, d, r: (d, 0, p))
    fine_spec = pl.BlockSpec(fine.shape, lambda p, d, r: (0, 0))
    coarse_spec = pl.BlockSpec(coarse.shape, lambda p, d, r: (0, 0))
    params = pltpu.CompilerParams(vmem_limit_bytes=48 * 1024 * 1024)
    spread = pl.pallas_call(
        functools.partial(spread_kernel, repeats=repeats),
        grid=steps,
        in_specs=[fields_spec, fine_spec, coarse_spec],
        out_specs=grid_spec,
        out_shape=jax.ShapeDtypeStruct((ZL, 2 * COLUMNS, GX), f32),
        compiler_params=params,
    )(gathered, fine, coarse)
    tile_spec = pl.BlockSpec((ZL, 2, TILE, GX), lambda t: (0, 0, t, 0))
    whole = lambda *shape: pl.BlockSpec(shape, lambda t: (0,) * len(shape))
    mixed = pl.pallas_call(
        functools.partial(mix_kernel, columns=columns),
        grid=(COLUMNS // TILE,),
        in_specs=[
            pl.BlockSpec(memory_space=pltpu.SMEM),
            pl.BlockSpec(memory_space=pltpu.SMEM),
            tile_spec,
            whole(*forward.shape),
            whole(*inverse.shape),
            whole(*twists.shape),
        ],
        out_specs=tile_spec,
        out_shape=jax.ShapeDtypeStruct((ZL, 2, COLUMNS, GX), f32),
        compiler_params=params,
    )(
        first.astype(jnp.int32).reshape(1),
        soil_scalars(soil),
        spread.reshape(ZL, 2, COLUMNS, GX),
        jnp.asarray(forward),
        jnp.asarray(inverse),
        jnp.asarray(twists),
    )
    partial = pl.pallas_call(
        sample_kernel,
        grid=steps,
        in_specs=[fields_spec, grid_spec, fine_spec, coarse_spec],
        out_specs=pl.BlockSpec(
            (1, 2, segments), lambda p, d, r: ((p * repeats + r) * depths + d, 0, 0)
        ),
        out_shape=jax.ShapeDtypeStruct((groups, 2, segments), f32),
        compiler_params=params,
    )(gathered, mixed.reshape(ZL, 2 * COLUMNS, GX), fine, coarse)
    arrived = lax.all_to_all(partial, ("pencil", "depth"), split_axis=0, concat_axis=0, tiled=True)
    far = jnp.sum(arrived, axis=0)

    own = lax.dynamic_index_in_dim(gathered, depth, axis=0, keepdims=False)
    beside = jnp.stack(
        [
            lax.dynamic_index_in_dim(
                own[:, 16:18], jnp.clip(pencil + step, 0, pencils - 1), axis=0, keepdims=False
            )
            for step in (-1, 0, 1)
        ]
    )
    return far + near_field(beside, near_pairs, corrections)


def solution(mesh):
    return jax.shard_map(
        shards,
        mesh=mesh,
        in_specs=(
            P(None, ("pencil", "depth")),
            P(None, ("pencil", "depth")),
            P(None, ("pencil", "depth")),
            P(),
            P(None, ("pencil", "depth")),
            P(("pencil", "depth"), None, None, None),
        ),
        out_specs=P(None, ("pencil", "depth")),
        check_vma=False,
    )
```

time: 1410 us -> 218 us (0.15); the launches traced: 1400 us -> 218 us
  local copies, waits for them, and re-layouts: 386 us -> 8.22 us
  matrix products: 344 us -> 8.45 us
  waiting for transfers between devices: 346 us -> 26.4 us
  blocking collectives: 189 us -> 21.9 us
  Pallas kernels: 0 us -> 137 us
  other arithmetic: 99.7 us -> 1.5 us
  starting transfers between devices: 24.6 us -> 8.64 us
    all_to_all x3 -> x2, waiting for transfers between devices: 285 us -> 26.4 us  [the longest x1 17.6 us: everyone(): return lax.all_to_all(copies, axis, split_axis=0, concat_axis=0, tiled=True)]
    dot_general x39 -> x7, matrix products: 253 us -> 8.45 us  [product(): return jnp.einsum(form, left, right, precision=highest)]
    all_to_all x1, blocking collectives: 189 us -> 21.9 us  [everyone(): return lax.all_to_all(copies, axis, split_axis=0, concat_axis=0, tiled=True)]
    pallas_call x0 -> x3, Pallas kernels: none -> 137 us  [the longest x1 60 us: shards(): pl.pallas_call(functools.partial(spread_kernel, repeats=repeats), grid=st...]
    another operation x15 -> x2, local copies, waits for them, and re-layouts: 95.2 us -> 2.6 us  [the longest x1 2.58 us: soil_scalars(): return jnp.stack([upper_re, upper_im, lower_re, lower_im, refl_re, refl_im])]
    dot_general x2 -> x0, matrix products: 90.9 us -> none  [the longest x1 46.8 us: shards(): lax.dot_general(stacked, column_select, (((1,), (1,)), ((), ())), precisi...]
    reshape x8 -> x1, local copies, waits for them, and re-layouts: 85.3 us -> 0.02 us  [near_field(): blocks = jnp.swapaxes(beside, 0, 1).reshape(2, slots, block_size)]
    squeeze x10 -> x2, local copies, waits for them, and re-layouts: 75.1 us -> 0.04 us  [the longest x1 0.04 us: shards(): own = lax.dynamic_index_in_dim(gathered, depth, axis=0, keepdims=False)]
  transfers between devices with their start and end apart: 5 -> 2, of which waited for: 4 -> 2; matrix products, arithmetic and copies ran while one was open for 1% -> 3% of each run, Pallas kernels for 0% -> 0%
where the time goes in v1:
time: 218 us
  Pallas kernels  137 us (63%)
  waiting for transfers between devices  26.4 us (12%)
  blocking collectives  21.9 us (10%)
  starting transfers between devices  8.64 us (4%)
  matrix products  8.45 us (4%)
  local copies, waits for them, and re-layouts  8.22 us (4%)
  between operations  5.23 us (2%)
    pallas_call x1, Pallas kernels, shards(): pl.pallas_call(functools.partial(spread_kernel, repeats=repeats), grid=st...  60 us
    pallas_call x1, Pallas kernels, shards(): pl.pallas_call(sample_kernel, grid=steps, in_specs=[fields_spec, grid_spe...  52.2 us
    pallas_call x1, Pallas kernels, shards(): pl.pallas_call(functools.partial(mix_kernel, columns=columns), grid=(COLU...  25.2 us
    all_to_all x1, blocking collectives, everyone(): return lax.all_to_all(copies, axis, split_axis=0, concat_axis=0, tiled=True)  21.9 us
    all_to_all x1, waiting for transfers between devices, everyone(): return lax.all_to_all(copies, axis, split_axis=0, concat_axis=0, tiled=True)  17.6 us
    all_to_all x1, waiting for transfers between devices, shards(): lax.all_to_all(partial, ('pencil', 'depth'), split_axis=0, concat_axis=0,...  8.81 us
    dot_general x7, matrix products, product(): return jnp.einsum(form, left, right, precision=highest)  8.45 us
    all_to_all x1, starting transfers between devices, everyone(): return lax.all_to_all(copies, axis, split_axis=0, concat_axis=0, tiled=True)  5.55 us
  transfers between devices with their start and end apart: 2, of which 2 were waited for; matrix products, arithmetic and copies ran while one was open for 3% of the time, Pallas kernels for 0%

profile of v1, /device:TPU:1, one launch (start us, length us, event | category | flops | bytes accessed | tf_op | source)
XLA Modules:
  0.0 217.7 jit_solution(16417662112673452957)
XLA Ops:
  0.0 0.8 slice_convert_fusion
  0.8 1.5 concatenate.4
  2.4 21.9 %all_to_all.15 = f32[8,24,768]{2,1,0:T(8,128)S(1)} all-to-all(f32[8,24,768]{2,1,0:T(8,128)S(1)} %broadcast_in_dim.7), channel_id=1, replica_groups=mesh['pencil'=8,'depth'=4] {'pencil'}, dimensions={0} | all-to-all | bytes 1179648 | tf_op jit(solution)/shard_map/all_to_all | solution.py:276
  24.3 1.6 broadcast_in_dim.8
  25.9 0.0 copy-start.4
  25.9 5.6 %all-to-all-start.1 = ((f32[4,8,24,768]{3,2,1,0:T(8,128)}), f32[4,8,24,768]{3,2,1,0:T(8,128)S(1)}, u32[]{:S(2)}, u32[]{:S(2)}) async-start(f32[4,8,24,768]{3,2,1,0:T(8,128)} %broadcast_in_dim.8), calls=%async_computation.1 | async-start | bytes 4718592 | tf_op jit(solution)/shard_map/all_to_all | solution.py:276
  31.4 0.0 copy-done.4
  31.4 0.7 fusion.37
  37.2 2.6 %stack.26.soil_ref = f32[6]{0:T(128)S(1)} concatenate(f32[1]{0:T(128)} %bitcast.1, f32[1]{0:T(128)} %bitcast.2, f32[1]{0:T(128)} %bitcast.3, f32[1]{0:T(128)} %bitcast.4, f32[1]{0:T(128)} %bitcast.5, f32[1]{0:T(128)} %bitcast.6), dimensions={0} | concatenate | bytes 48 | tf_op jit(solution)/shard_map/stack | solution.py:308
  39.8 0.8 constant_dynamic-slice_fusion.4
  40.5 0.9 constant_dynamic-slice_fusion.3
  41.5 0.0 copy-done.5
  41.5 17.6 %all-to-all-done.1.fields_ref = f32[4,8,24,768]{3,2,1,0:T(8,128)S(1)} async-done(((f32[4,8,24,768]{3,2,1,0:T(8,128)}), f32[4,8,24,768]{3,2,1,0:T(8,128)S(1)}, u32[]{:S(2)}, u32[]{:S(2)}) %all-to-all-start.1) | async-done | bytes 2359328 | tf_op jit(solution)/shard_map/all_to_all | solution.py:276
  59.2 0.0 copy-start.3
  59.2 0.2 convolution_bitcast_fusion
  59.4 2.6 %fusion.4 = f32[12,1,128]{2,1,0:T(1,128)S(1)} fusion(f32[12,2,128,128]{3,2,1,0:T(8,128)} %param.16, f32[12,128,1]{1,0,2:T(8,128)S(1)} %get-tuple-element.8), kind=kOutput, calls=%fused_computation.7 | convolution fusion | flops 2359296 | bytes 798720 | tf_op jit(solution)/shard_map/pij,pj->pi/dot_general | solution.py:32
  62.0 2.5 %fusion.2 = f32[12,1,128]{2,1,0:T(1,128)S(1)} fusion(f32[12,2,128,128]{3,2,1,0:T(8,128)} %param.16, f32[12,128,1]{1,0,2:T(8,128)S(1)} %get-tuple-element.8), kind=kOutput, calls=%fused_computation.5 | convolution fusion | flops 2359296 | bytes 798720 | tf_op jit(solution)/shard_map/pij,pj->pi/dot_general | solution.py:32
  64.5 0.0 copy-done.3
  64.5 1.3 fusion
  65.8 1.3 fusion.6
  67.2 60.0 %shard_map.109 = f32[8,128,2048]{2,1,0:T(8,128)} custom-call(f32[4,8,24,768]{3,2,1,0:T(8,128)S(1)} %all-to-all-done.1.fields_ref, bf16[128,48]{1,0:T(8,128)(2,1)S(1)} %bitcast.71, bf16[128,512]{1,0:T(8,128)(2,1)S(1)} %bitcast.69), custom_call_target="tpu_custom_call" | custom-call | tf_op jit(solution)/shard_map/pallas_call | solution.py:353
  127.2 0.0 copy-done
  127.2 0.0 copy-done.1
  127.2 0.0 copy-done.2
  127.2 25.2 %shard_map.110 = f32[8,2,64,2048]{3,2,1,0:T(8,128)} custom-call(s32[1]{0:T(128)} %bitcast.first_ref, f32[6]{0:T(128)S(1)} %stack.26.soil_ref, f32[8,2,64,2048]{3,2,1,0:T(8,128)} %bitcast.74, bf16[2,512,512]{2,1,0:T(8,128)(2,1)S(1)} %copy-done, bf16[2,512,512]{2,1,0:T(8,128)(2,1)S(1)} %copy-done.1, f32[2,8,256]{2,1,0:T(8,128)S(1)} %copy-done.2), custom_call_target="tpu_custom_call" | custom-call | tf_op jit(solution)/shard_map/pallas_call | solution.py:363
  152.3 52.2 %shard_map.111 = f32[32,2,768]{2,1,0:T(2,128)} custom-call(f32[4,8,24,768]{3,2,1,0:T(8,128)S(1)} %all-to-all-done.1.fields_ref, f32[8,128,2048]{2,1,0:T(8,128)} %bitcast.73, bf16[128,48]{1,0:T(8,128)(2,1)S(1)} %bitcast.72, bf16[128,512]{1,0:T(8,128)(2,1)S(1)} %bitcast.70), custom_call_target="tpu_custom_call" | custom-call | tf_op jit(solution)/shard_map/pallas_call | solution.py:385
  204.6 3.1 %all-to-all-start.2 = ((f32[32,2,768]{2,1,0:T(2,128)}), f32[32,2,768]{2,1,0:T(2,128)S(1)}, u32[]{:S(2)}, u32[]{:S(2)}) async-start(f32[32,2,768]{2,1,0:T(2,128)} %shard_map.111), calls=%async_computation.2 | async-start | bytes 393216 | tf_op jit(solution)/shard_map/all_to_all | solution.py:395
  207.7 0.3 convolution_bitcast_fusion.1
  207.9 0.3 convolution_bitcast_fusion.2
  208.2 8.8 %all-to-all-done.2 = f32[32,2,768]{2,1,0:T(2,128)S(1)} async-done(((f32[32,2,768]{2,1,0:T(2,128)}), f32[32,2,768]{2,1,0:T(2,128)S(1)}, u32[]{:S(2)}, u32[]{:S(2)}) %all-to-all-start.2) | async-done | bytes 196640 | tf_op jit(solution)/shard_map/all_to_all | solution.py:395
  217.0 0.1 reduce_sum.9
  217.1 0.6 maximum_add_fusion
  (15 shorter events, 0.2 us)
Async XLA Ops:
  25.9 5.6 %copy-start.4 = (f32[2,2]{1,0:T(2,128)S(1)}, f32[2,2]{1,0:T(2,128)}, u32[]{:S(2)}) copy-start(f32[2,2]{1,0:T(2,128)} %param.14) | copy-start | bytes 52
  25.9 15.6 %copy-start.5 = (s32[3,12]{1,0:T(4,128)S(1)}, s32[3,12]{1,0:T(4,128)}, u32[]{:S(2)}) copy-start(s32[3,12]{1,0:T(4,128)} %param.15) | copy-start | bytes 436
  25.9 33.2 %all-to-all-start.1 = ((f32[4,8,24,768]{3,2,1,0:T(8,128)}), f32[4,8,24,768]{3,2,1,0:T(8,128)S(1)}, u32[]{:S(2)}, u32[]{:S(2)}) async-start(f32[4,8,24,768]{3,2,1,0:T(8,128)} %broadcast_in_dim.8), calls=%async_computation.1 | async-start | bytes 4718592 | tf_op jit(solution)/shard_map/all_to_all | solution.py:276
  59.2 5.2 %copy-start.3 = (f32[12,2,128,128]{3,2,1,0:T(8,128)S(1)}, f32[12,2,128,128]{3,2,1,0:T(8,128)}, u32[]{:S(2)}) copy-start(f32[12,2,128,128]{3,2,1,0:T(8,128)} %param.16) | copy-start | bytes 4718596
  67.1 60.0 %copy-start = (bf16[2,512,512]{2,1,0:T(8,128)(2,1)S(1)}, bf16[2,512,512]{2,1,0:T(8,128)(2,1)}, u32[]{:S(2)}) copy-start(bf16[2,512,512]{2,1,0:T(8,128)(2,1)} %constant.90.clone.forward_ref) | copy-start | bytes 3145732
  67.2 60.0 %copy-start.1 = (bf16[2,512,512]{2,1,0:T(8,128)(2,1)S(1)}, bf16[2,512,512]{2,1,0:T(8,128)(2,1)}, u32[]{:S(2)}) copy-start(bf16[2,512,512]{2,1,0:T(8,128)(2,1)} %constant.91.clone.inverse_ref) | copy-start | bytes 3145732
  67.2 60.0 %copy-start.2 = (f32[2,8,256]{2,1,0:T(8,128)S(1)}, f32[2,8,256]{2,1,0:T(8,128)}, u32[]{:S(2)}) copy-start(f32[2,8,256]{2,1,0:T(8,128)} %constant.92.clone.twist_ref) | copy-start | bytes 49156
  204.6 12.5 %all-to-all-start.2 = ((f32[32,2,768]{2,1,0:T(2,128)}), f32[32,2,768]{2,1,0:T(2,128)S(1)}, u32[]{:S(2)}, u32[]{:S(2)}) async-start(f32[32,2,768]{2,1,0:T(2,128)} %shard_map.111), calls=%async_computation.2 | async-start | bytes 393216 | tf_op jit(solution)/shard_map/all_to_all | solution.py:395

commit v2 on v1

--- a/solution.py
+++ b/solution.py
@@ -15,7 +15,8 @@
 ZL = 8
 
 LANES = 256
-RADIX = GX // LANES
+INNER = 128
+RADIX = GX // INNER
 FINE = 8
 SPAN = 16
 COLUMNS = 64
@@ -58,8 +59,8 @@
 
 
 def transform_tables():
-    index = np.arange(LANES)
-    phase = (index[:, None] * index[None, :] % LANES) * (2.0 * math.pi / LANES)
+    index = np.arange(INNER)
+    phase = (index[:, None] * index[None, :] % INNER) * (2.0 * math.pi / INNER)
     cos, sin = np.cos(phase), np.sin(phase)
     forward = np.block([[cos, -sin], [sin, cos]])
     twist = (np.arange(RADIX)[:, None] * index[None, :]) * (2.0 * math.pi / GX)
@@ -67,11 +68,15 @@
     return np.stack(host_halves(forward)), np.stack(host_halves(forward.T)), twists
 
 
+def one_hot(index, size):
+    candidate = lax.broadcasted_iota(jnp.int16, (size, index.shape[1]), 0)
+    return jnp.where(candidate == index.astype(jnp.int16), bf16(1), bf16(0))
+
+
 def segment_factors(fields, fine_ref, coarse_ref):
     count = fields.shape[1]
     column = fields[19:20].astype(jnp.int32)
-    coarse_index = lax.broadcasted_iota(jnp.int32, (GY // FINE, count), 0)
-    pick = jnp.where(coarse_index == column // FINE, 1.0, 0.0).astype(bf16)
+    pick = one_hot(column // FINE, GY // FINE)
     coarse = jnp.dot(
         coarse_ref[...], jnp.concatenate([pick, pick], axis=0), preferred_element_type=f32
     )
@@ -89,13 +94,7 @@
     return coarse, fines
 
 
-def row_select(fields, total_rows):
-    row = fields[18:19].astype(jnp.int32)
-    row_index = lax.broadcasted_iota(jnp.int32, (total_rows, fields.shape[1]), 0)
-    return jnp.where(row_index == row, 1.0, 0.0).astype(bf16)
-
-
-def spread_kernel(fields_ref, fine_ref, coarse_ref, out_ref, *, repeats):
+def spread_kernel(place_ref, before_ref, fields_ref, fine_ref, coarse_ref, out_ref, *, repeats):
     fields = fields_ref[0]
     layers = out_ref.shape[0]
     coarse, fines = segment_factors(fields, fine_ref, coarse_ref)
@@ -108,17 +107,11 @@
         fine_re, fine_im = fine[:COLUMNS], fine[COLUMNS:]
         parts.append(halves(wave_re * fine_re - wave_im * fine_im))
         parts.append(halves(wave_re * fine_im + wave_im * fine_re))
-    select = row_select(fields, layers * LANES)
+    factors = jnp.concatenate([part[i] for i in range(2) for part in parts], axis=0)
+    select = one_hot(fields[18:19].astype(jnp.int32), layers * LANES)
     form = (((1,), (1,)), ((), ()))
-    spread = sum(
-        lax.dot_general(
-            jnp.concatenate([part[i] for part in parts], axis=0),
-            select,
-            form,
-            preferred_element_type=f32,
-        )
-        for i in range(2)
-    )
+    spread = lax.dot_general(factors, select, form, preferred_element_type=f32)
+    spread = spread[: 8 * COLUMNS] + spread[8 * COLUMNS :]
     total = spread[: 2 * COLUMNS]
     for a in range(1, 4):
         total = total + pltpu.roll(spread[2 * COLUMNS * a : 2 * COLUMNS * (a + 1)], a, 1)
@@ -127,28 +120,23 @@
         if repeats == 1:
             out_ref[layer] = piece
         else:
-            fresh = pl.program_id(2) == 0
-            out_ref[layer] = jnp.where(fresh, 0.0, out_ref[layer]) + piece
-
-
-def sample_kernel(fields_ref, field_ref, fine_ref, coarse_ref, out_ref):
+            fresh = pl.program_id(0) % min(repeats, pl.num_programs(0)) == 0
+            out_ref[layer] = jnp.where(fresh, before_ref[layer], out_ref[layer]) + piece
+
+
+def sample_kernel(place_ref, before_ref, fields_ref, field_ref, fine_ref, coarse_ref, out_ref):
     fields = fields_ref[0]
     layers = field_ref.shape[0]
     total_rows = layers * LANES
     coarse, fines = segment_factors(fields, fine_ref, coarse_ref)
-    select = row_select(fields, total_rows)
+    select = one_hot(fields[18:19].astype(jnp.int32), total_rows)
     field = jnp.concatenate([field_ref[layer] for layer in range(layers)], axis=1)
     parts = [halves(field)]
     for a in range(1, 4):
         parts.append(halves(pltpu.roll(field, total_rows - a, 1)))
-    sampled = sum(
-        jnp.dot(
-            jnp.concatenate([part[i] for part in parts], axis=0),
-            select,
-            preferred_element_type=f32,
-        )
-        for i in range(2)
-    )
+    factors = jnp.concatenate([part[i] for i in range(2) for part in parts], axis=0)
+    sampled = jnp.dot(factors, select, preferred_element_type=f32)
+    sampled = sampled[: 8 * COLUMNS] + sampled[8 * COLUMNS :]
     sum_re, sum_im = 0.0, 0.0
     for a, fine in enumerate(fines):
         fine_re, fine_im = fine[:COLUMNS], fine[COLUMNS:]
@@ -165,19 +153,18 @@
 
 def turn(value, step, size, sign):
     real, imag = value
-    eighth = step * (8 // size)
-    if eighth == 0:
+    if step == 0:
         return value
-    if eighth == 2:
-        return (-sign * imag, sign * real) if sign > 0 else (imag, -real)
+    if 4 * step == size:
+        return (-imag, real) if sign > 0 else (imag, -real)
     half = math.sqrt(0.5)
-    if eighth == 1:
+    if 8 * step == size:
         if sign > 0:
             return ((real - imag) * half, (real + imag) * half)
         return ((real + imag) * half, (imag - real) * half)
-    if sign > 0:
-        return ((real + imag) * -half, (real - imag) * half)
-    return ((imag - real) * half, (real + imag) * -half)
+    cos = math.cos(2.0 * math.pi * step / size)
+    sin = sign * math.sin(2.0 * math.pi * step / size)
+    return (real * cos - imag * sin, real * sin + imag * cos)
 
 
 def butterflies(values, sign):
@@ -203,10 +190,9 @@
     )
 
 
-def mix(spec, kappa, keep, soil_ref):
-    upper = (soil_ref[0], soil_ref[1])
-    lower = (soil_ref[2], soil_ref[3])
-    refl_re, refl_im = soil_ref[4], soil_ref[5]
+def mix(spec, kappa, keep, soil_ref, reflection):
+    upper = (soil_ref[0, 0], soil_ref[1, 0])
+    lower = (soil_ref[0, 1], soil_ref[1, 1])
     decay = jnp.exp(-kappa)
     base = jnp.where(keep, 1.0 / (GX * GY) / (kappa + screening), 0.0)
     source = []
@@ -220,8 +206,8 @@
         below[layer] = tuple(decay * (below[layer + 1][i] + source[layer + 1][i]) for i in range(2))
     surface = tuple(decay * (below[0][i] + source[0][i]) for i in range(2))
     image = (
-        refl_re * surface[0] - refl_im * surface[1],
-        refl_re * surface[1] + refl_im * surface[0],
+        reflection[0] * surface[0] - reflection[1] * surface[1],
+        reflection[0] * surface[1] + reflection[1] * surface[0],
     )
     above = source[0]
     mixed = []
@@ -233,18 +219,31 @@
     return mixed
 
 
-def mix_kernel(first_ref, soil_ref, spec_ref, forward_ref, inverse_ref, twist_ref, out_ref, *, columns):
+def reflect(soil_ref, shape):
+    upper_re, lower_re = (jnp.full(shape, soil_ref[0, i], f32) for i in range(2))
+    upper_im, lower_im = (jnp.full(shape, soil_ref[1, i], f32) for i in range(2))
+    denom_re, denom_im = upper_re + lower_re, upper_im + lower_im
+    numer_re, numer_im = lower_re - upper_re, lower_im - upper_im
+    magnitude = denom_re * denom_re + denom_im * denom_im
+    return (
+        (numer_re * denom_re + numer_im * denom_im) / magnitude,
+        (numer_im * denom_re - numer_re * denom_im) / magnitude,
+    )
+
+
+def mix_kernel(place_ref, soil_ref, spec_ref, forward_ref, inverse_ref, twist_ref, out_ref, *, columns):
     tile = spec_ref.shape[2]
     rows = ZL * tile
     real = spec_ref[:, 0].reshape(rows, GX)
     imag = spec_ref[:, 1].reshape(rows, GX)
-    cut = [slice(n * LANES, (n + 1) * LANES) for n in range(RADIX)]
+    cut = [slice(n * INNER, (n + 1) * INNER) for n in range(RADIX)]
     values = butterflies([(real[:, c], imag[:, c]) for c in cut], -1.0)
-    local = pl.program_id(0) * tile + lax.broadcasted_iota(jnp.int32, (tile, LANES), 0)
+    local = pl.program_id(0) * tile + lax.broadcasted_iota(jnp.int32, (tile, INNER), 0)
     keep = local < columns
-    ky = first_ref[0] + local
+    ky = place_ref[2] + local
+    reflection = reflect(soil_ref, (tile, INNER))
     freq_y = jnp.where(ky < (GY - 1) // 2 + 1, ky, ky - GY).astype(f32) / GY
-    inner = lax.broadcasted_iota(jnp.int32, (tile, LANES), 1)
+    inner = lax.broadcasted_iota(jnp.int32, (tile, INNER), 1)
     back = []
     for k in range(RADIX):
         twist_re, twist_im = twist_ref[0, k : k + 1], twist_ref[1, k : k + 1]
@@ -255,25 +254,24 @@
         freq_x = jnp.where(kx < (GX - 1) // 2 + 1, kx, kx - GX).astype(f32) / GX
         kappa = 2.0 * math.pi * jnp.sqrt(freq_x * freq_x + freq_y * freq_y)
         spec = [
-            (spectrum[s * tile : (s + 1) * tile, :LANES], spectrum[s * tile : (s + 1) * tile, LANES:])
+            (spectrum[s * tile : (s + 1) * tile, :INNER], spectrum[s * tile : (s + 1) * tile, INNER:])
             for s in range(ZL)
         ]
-        mixed = mix(spec, kappa, keep, soil_ref)
+        mixed = mix(spec, kappa, keep, soil_ref, reflection)
         stacked = jnp.concatenate([jnp.concatenate(pair, axis=1) for pair in mixed], axis=0)
         field = dense(stacked, inverse_ref)
-        re, im = field[:, :LANES], field[:, LANES:]
+        re, im = field[:, :INNER], field[:, INNER:]
         turned = (re * twist_re + im * twist_im, im * twist_re - re * twist_im) if k else (re, im)
         back.append(turned)
     values = butterflies(back, 1.0)
     for n in range(RADIX):
-        out_ref[:, 0, :, cut[n]] = values[n][0].reshape(ZL, tile, LANES)
-        out_ref[:, 1, :, cut[n]] = values[n][1].reshape(ZL, tile, LANES)
-
-
-def everyone(value, axis):
+        out_ref[:, 0, :, cut[n]] = values[n][0].reshape(ZL, tile, INNER)
+        out_ref[:, 1, :, cut[n]] = values[n][1].reshape(ZL, tile, INNER)
+
+
+def partner(value, axis, step):
     count = lax.axis_size(axis)
-    copies = jnp.broadcast_to(value[None], (count,) + value.shape)
-    return lax.all_to_all(copies, axis, split_axis=0, concat_axis=0, tiled=True)
+    return lax.ppermute(value, axis, [(i, i ^ step) for i in range(count)])
 
 
 def near_field(beside, near_pairs, corrections):
@@ -295,17 +293,6 @@
     ) * live.astype(f32)[:, None]
     near = jnp.stack([product("pt,pi->ti", owner, piece_re), product("pt,pi->ti", owner, piece_im)])
     return near.reshape(2, block_count * block_size)
-
-
-def soil_scalars(soil):
-    upper_re, lower_re = (soil[0, 0], soil[0, 1])
-    upper_im, lower_im = (soil[1, 0], soil[1, 1])
-    denom_re, denom_im = upper_re + lower_re, upper_im + lower_im
-    numer_re, numer_im = lower_re - upper_re, lower_im - upper_im
-    magnitude = denom_re * denom_re + denom_im * denom_im
-    refl_re = (numer_re * denom_re + numer_im * denom_im) / magnitude
-    refl_im = (numer_im * denom_re - numer_re * denom_im) / magnitude
-    return jnp.stack([upper_re, upper_im, lower_re, lower_im, refl_re, refl_im])
 
 
 def shards(currents, stencil_cells, stencil_weights, soil, near_pairs, corrections):
@@ -331,7 +318,14 @@
             jnp.zeros((FIELDS - 20, segments), f32),
         ]
     )
-    gathered = everyone(everyone(fields, "pencil"), "depth")
+    bits = [1 << i for i in range(pencils.bit_length() - 1)]
+    if repeats == 1:
+        bits = bits[::-1]
+    place = jnp.stack([pencil, depth, first]).astype(jnp.int32)
+
+    def offset(index):
+        return sum((index >> j & 1) * bit for j, bit in enumerate(bits))
+
 
     fine, coarse = column_tables()
     fine = lax.dynamic_slice_in_dim(
@@ -341,23 +335,73 @@
         jnp.asarray(np.pad(coarse, ((0, 0), (0, COLUMNS), (0, 0)))), first, COLUMNS, axis=1
     ).reshape(2 * COLUMNS, -1)
     forward, inverse, twists = transform_tables()
-
-    steps = (GX // LANES, depths, repeats)
-    fields_spec = pl.BlockSpec(
-        (None, 1, FIELDS, segments), lambda p, d, r: (d, p * repeats + r, 0, 0)
-    )
-    grid_spec = pl.BlockSpec((layers, 2 * COLUMNS, LANES), lambda p, d, r: (d, 0, p))
-    fine_spec = pl.BlockSpec(fine.shape, lambda p, d, r: (0, 0))
-    coarse_spec = pl.BlockSpec(coarse.shape, lambda p, d, r: (0, 0))
     params = pltpu.CompilerParams(vmem_limit_bytes=48 * 1024 * 1024)
-    spread = pl.pallas_call(
-        functools.partial(spread_kernel, repeats=repeats),
-        grid=steps,
-        in_specs=[fields_spec, fine_spec, coarse_spec],
-        out_specs=grid_spec,
-        out_shape=jax.ShapeDtypeStruct((ZL, 2 * COLUMNS, GX), f32),
-        compiler_params=params,
-    )(gathered, fine, coarse)
+    fields_spec = pl.BlockSpec((1, FIELDS, segments), lambda i, place: (i, 0, 0))
+
+    def region(begin, step):
+        return pl.BlockSpec(
+            (layers, 2 * COLUMNS, LANES),
+            lambda i, place: (place[1] ^ step, 0, (place[0] ^ offset(begin + i)) // repeats),
+        )
+
+    fine_spec = pl.BlockSpec(fine.shape, lambda i, place: (0, 0))
+    coarse_spec = pl.BlockSpec(coarse.shape, lambda i, place: (0, 0))
+    anywhere = pl.BlockSpec(memory_space=pl.ANY)
+
+    def cost(blocks):
+        return pl.CostEstimate(
+            flops=blocks * 2_000_000_000, bytes_accessed=blocks * 600_000, transcendentals=0
+        )
+
+    def spread(grid, chunk, begin, step):
+        fresh = grid is None
+        if fresh and repeats > 1:
+            grid, fresh = jnp.zeros((ZL, 2 * COLUMNS, GX), f32), False
+        before = jnp.zeros((8, 128), f32) if fresh else grid
+        return pl.pallas_call(
+            functools.partial(spread_kernel, repeats=repeats),
+            grid_spec=pltpu.PrefetchScalarGridSpec(
+                num_scalar_prefetch=1,
+                grid=(chunk.shape[0],),
+                in_specs=[
+                    anywhere if repeats == 1 else region(begin, step),
+                    fields_spec,
+                    fine_spec,
+                    coarse_spec,
+                ],
+                out_specs=region(begin, step),
+            ),
+            out_shape=jax.ShapeDtypeStruct((ZL, 2 * COLUMNS, GX), f32),
+            input_output_aliases={} if fresh else {1: 0},
+            compiler_params=params,
+            cost_estimate=cost(chunk.shape[0]),
+        )(place, before, chunk, fine, coarse)
+
+    ends = [(i, i + 1) for i in range(pencils - 1)]
+    beside = jnp.stack(
+        [
+            lax.ppermute(currents, "pencil", ends),
+            currents,
+            lax.ppermute(currents, "pencil", [(j, i) for i, j in ends]),
+        ]
+    )
+    own, grid = fields[None], None
+    for number, bit in enumerate(bits):
+        arrived = partner(own, "pencil", bit)
+        own = jnp.concatenate([own, arrived])
+        if number == 0:
+            grid = spread(grid, own, 0, 0)
+        else:
+            grid = spread(grid, arrived, 1 << number, 0)
+    parts = [own]
+    for step in range(1, depths):
+        low = step & -step
+        parts.append(partner(parts[step ^ low], "depth", low))
+    near = near_field(beside, near_pairs, corrections)
+    near, parts[1] = lax.optimization_barrier((near, parts[1]))
+    for step in range(1, depths):
+        grid = spread(grid, parts[step], 0, step)
+
     tile_spec = pl.BlockSpec((ZL, 2, TILE, GX), lambda t: (0, 0, t, 0))
     whole = lambda *shape: pl.BlockSpec(shape, lambda t: (0,) * len(shape))
     mixed = pl.pallas_call(
@@ -375,36 +419,44 @@
         out_shape=jax.ShapeDtypeStruct((ZL, 2, COLUMNS, GX), f32),
         compiler_params=params,
     )(
-        first.astype(jnp.int32).reshape(1),
-        soil_scalars(soil),
-        spread.reshape(ZL, 2, COLUMNS, GX),
+        place,
+        soil,
+        grid.reshape(ZL, 2, COLUMNS, GX),
         jnp.asarray(forward),
         jnp.asarray(inverse),
         jnp.asarray(twists),
-    )
-    partial = pl.pallas_call(
-        sample_kernel,
-        grid=steps,
-        in_specs=[fields_spec, grid_spec, fine_spec, coarse_spec],
-        out_specs=pl.BlockSpec(
-            (1, 2, segments), lambda p, d, r: ((p * repeats + r) * depths + d, 0, 0)
-        ),
-        out_shape=jax.ShapeDtypeStruct((groups, 2, segments), f32),
-        compiler_params=params,
-    )(gathered, mixed.reshape(ZL, 2 * COLUMNS, GX), fine, coarse)
+    ).reshape(ZL, 2 * COLUMNS, GX)
+    partial = None
+    for step in range(depths):
+        partial = pl.pallas_call(
+            sample_kernel,
+            grid_spec=pltpu.PrefetchScalarGridSpec(
+                num_scalar_prefetch=1,
+                grid=(pencils,),
+                in_specs=[anywhere, fields_spec, region(0, step), fine_spec, coarse_spec],
+                out_specs=pl.BlockSpec(
+                    (1, 2, segments),
+                    lambda i, place, step=step: (
+                        (place[0] ^ offset(i)) * depths + (place[1] ^ step),
+                        0,
+                        0,
+                    ),
+                ),
+            ),
+            out_shape=jax.ShapeDtypeStruct((groups, 2, segments), f32),
+            input_output_aliases={1: 0} if step else {},
+            compiler_params=params,
+            cost_estimate=cost(pencils),
+        )(
+            place,
+            partial if step else jnp.zeros((8, 128), f32),
+            parts[step],
+            mixed,
+            fine,
+            coarse,
+        )
     arrived = lax.all_to_all(partial, ("pencil", "depth"), split_axis=0, concat_axis=0, tiled=True)
-    far = jnp.sum(arrived, axis=0)
-
-    own = lax.dynamic_index_in_dim(gathered, depth, axis=0, keepdims=False)
-    beside = jnp.stack(
-        [
-            lax.dynamic_index_in_dim(
-                own[:, 16:18], jnp.clip(pencil + step, 0, pencils - 1), axis=0, keepdims=False
-            )
-            for step in (-1, 0, 1)
-        ]
-    )
-    return far + near_field(beside, near_pairs, corrections)
+    return jnp.sum(arrived, axis=0) + near
 
 
 def solution(mesh):

time: 218 us -> 169 us (0.78)
  waiting for transfers between devices: 26.4 us -> 1.38 us
  Pallas kernels: 137 us -> 126 us
  blocking collectives: 21.9 us -> 11.7 us
  starting transfers between devices: 8.64 us -> 15.3 us
  between operations: 5.23 us -> 0.15 us
  local copies, waits for them, and re-layouts: 8.22 us -> 3.27 us
    all_to_all x2 -> x0, waiting for transfers between devices: 26.4 us -> none  [the longest x1 17.6 us: everyone(): return lax.all_to_all(copies, axis, split_axis=0, concat_axis=0, tiled=True)]
    ppermute x0 -> x8, starting transfers between devices: none -> 15.3 us  [the longest x6 9.27 us: partner(): return lax.ppermute(value, axis, [(i, i ^ step) for i in range(count)])]
    all_to_all x1, blocking collectives: 21.9 us -> 11.7 us  [shards(): lax.all_to_all(partial, ('pencil', 'depth'), split_axis=0, concat_axis=0,...]
    pallas_call x1, Pallas kernels: 25.2 us -> 16.2 us  [shards(): pl.pallas_call(functools.partial(mix_kernel, columns=columns), grid=(COLU...]
    all_to_all x2 -> x0, starting transfers between devices: 8.64 us -> none  [the longest x1 5.55 us: everyone(): return lax.all_to_all(copies, axis, split_axis=0, concat_axis=0, tiled=True)]
    another operation x1, local copies, waits for them, and re-layouts: 2.58 us -> 0.01 us  [soil_scalars(): return jnp.stack([upper_re, upper_im, lower_re, lower_im, refl_re, refl_im])]
    pallas_call x2 -> x10, Pallas kernels: 112 us -> 110 us  [the longest x6 58.5 us: spread(): pl.pallas_call(functools.partial(spread_kernel, repeats=repeats), grid_sp...]
  transfers between devices with their start and end apart: 2 -> 8, of which waited for: 2 -> 1; matrix products, arithmetic and copies ran while one was open for 3% -> 8% of each run, Pallas kernels for 0% -> 26%
where the time goes in v2:
time: 169 us
  Pallas kernels  126 us (75%)
  starting transfers between devices  15.3 us (9%)
  blocking collectives  11.7 us (7%)
  matrix products  7.23 us (4%)
  local copies, waits for them, and re-layouts  3.27 us (2%)
  other arithmetic  3.16 us (2%)
    pallas_call x6, Pallas kernels, spread(): pl.pallas_call(functools.partial(spread_kernel, repeats=repeats), grid_sp...  58.5 us
    pallas_call x4, Pallas kernels, shards(): pl.pallas_call(sample_kernel, grid_spec=pltpu.PrefetchScalarGridSpec(num_...  51.8 us
    pallas_call x1, Pallas kernels, shards(): pl.pallas_call(functools.partial(mix_kernel, columns=columns), grid=(COLU...  16.2 us
    all_to_all x1, blocking collectives, shards(): lax.all_to_all(partial, ('pencil', 'depth'), split_axis=0, concat_axis=0,...  11.7 us
    ppermute x6, starting transfers between devices, partner(): return lax.ppermute(value, axis, [(i, i ^ step) for i in range(count)])  9.27 us
    dot_general x7, matrix products, product(): return jnp.einsum(form, left, right, precision=highest)  7.23 us
    ppermute x1, starting transfers between devices, shards(): lax.ppermute(currents, 'pencil', ends)  4.61 us
  transfers between devices with their start and end apart: 8, of which 1 were waited for; matrix products, arithmetic and copies ran while one was open for 8% of the time, Pallas kernels for 26%

profile of v2, /device:TPU:1, one launch (start us, length us, event | category | flops | bytes accessed | tf_op | source)
XLA Modules:
  0.0 168.6 jit_solution(8362758719369763037)
XLA Ops:
  0.0 1.4 collective-permute-start.4
  1.4 4.6 %collective-permute-start.3 = (f32[2,768]{1,0:T(2,128)}, f32[2,768]{1,0:T(2,128)S(1)}, u32[]{:S(2)}, u32[]{:S(2)}) collective-permute-start(f32[2,768]{1,0:T(2,128)} %param.11), channel_id=1, source_target_pairs={{0,4},{4,8},{8,12},{12,16},{16,20},{20,24},{24,28},{1,5},{5,9},{9,... | collective-permute-start | bytes 18440 | tf_op jit(solution)/shard_map/ppermute | solution.py:383
  6.0 0.8 slice_convert_fusion
  6.8 1.5 concatenate.15
  8.4 2.6 %collective-permute-start = (f32[1,24,768]{2,1,0:T(8,128)S(1)}, f32[1,24,768]{2,1,0:T(8,128)S(1)}, u32[]{:S(2)}, u32[]{:S(2)}) collective-permute-start(f32[1,24,768]{2,1,0:T(8,128)S(1)} %bitcast.92), channel_id=1, source_target_pairs={{0,16},{4,20},{8,24},{12,28},{16,0},{20,4},{24,8},{28,12},{1,17},{... | collective-permute-start | bytes 221192 | tf_op jit(solution)/shard_map/ppermute | solution.py:274
  11.0 0.9 constant_dynamic-slice_fusion
  11.9 0.8 constant_dynamic-slice_fusion.1
  12.7 0.8 slice_bitcast_fusion.3
  13.5 0.7 maximum_bitcast_fusion
  14.5 2.5 %fusion.4 = f32[12,1,128]{2,1,0:T(1,128)S(1)} fusion(f32[12,2,128,128]{3,2,1,0:T(8,128)} %param.16, f32[12,128,1]{1,0,2:T(8,128)S(1)} %get-tuple-element.9), kind=kOutput, calls=%fused_computation.7 | convolution fusion | flops 2359296 | bytes 798720 | tf_op jit(solution)/shard_map/pij,pj->pi/dot_general | solution.py:33
  16.9 1.3 fusion.2
  18.3 1.3 fusion
  19.6 1.3 fusion.6
  21.6 1.4 collective-permute-start.1
  22.9 4.6 %shard_map.109.before_ref = f32[8,128,2048]{2,1,0:T(8,128)} custom-call(s32[3]{0:T(128)S(1)} %pad_add_fusion.place_ref, f32[8,128]{1,0:T(8,128)S(1)} %broadcast_3_before_ref.2.before_ref, f32[2,24,768]{2,1,0:T(8,128)S(1)} %pad_maximum_fusion.2.fields_ref, bf16[128,48]{1,0:T(8,128)(2,1)S(1)} %bitcast.77, bf16[128,512]{1,0:T(8,128)(2,1)S(1)} %bitcast.67), custom_call_target="tpu_custom_call" | custom-call | flops 4000000000 | bytes 1200000 | tf_op jit(solution)/shard_map/pallas_call | solution.py:361
  27.6 0.9 collective-permute-start.2
  28.6 4.4 %shard_map.110.before_ref = f32[8,128,2048]{2,1,0:T(8,128)} custom-call(s32[3]{0:T(128)S(1)} %pad_add_fusion.place_ref, f32[8,128,2048]{2,1,0:T(8,128)} %shard_map.109.before_ref, f32[2,24,768]{2,1,0:T(8,128)S(1)} %collective-permute-done.1.fields_ref, bf16[128,48]{1,0:T(8,128)(2,1)S(1)} %bitcast.78, ...), custom_call_target="tpu_custom_call", output_to_operand_aliasing={{}: (1, {})} | custom-call | flops 4000000000 | bytes 1200000 | tf_op jit(solution)/shard_map/pallas_call | solution.py:361
  33.0 1.4 collective-permute-done.2.fields_ref
  34.4 2.8 %collective-permute-start.5 = (f32[8,24,768]{2,1,0:T(8,128)S(1)}, f32[8,24,768]{2,1,0:T(8,128)S(1)}, u32[]{:S(2)}, u32[]{:S(2)}) collective-permute-start(f32[8,24,768]{2,1,0:T(8,128)S(1)} %pad_maximum_fusion.fields_ref), channel_id=1, source_target_pairs={{0,1},{1,0},{2,3},{3,2},{4,5},{5,4},{6,7},{7,6},{8,9},{9,8},{10,11... | collective-permute-start | bytes 1769480 | tf_op jit(solution)/shard_map/ppermute | solution.py:274
  37.2 1.2 collective-permute-start.6
  38.4 7.6 %shard_map.111.before_ref = f32[8,128,2048]{2,1,0:T(8,128)} custom-call(s32[3]{0:T(128)S(1)} %pad_add_fusion.place_ref, f32[8,128,2048]{2,1,0:T(8,128)} %shard_map.110.before_ref, f32[4,24,768]{2,1,0:T(8,128)S(1)} %collective-permute-done.2.fields_ref, bf16[128,48]{1,0:T(8,128)(2,1)S(1)} %bitcast.79, ...), custom_call_target="tpu_custom_call", output_to_operand_aliasing={{}: (1, {})} | custom-call | flops 8000000000 | bytes 2400000 | tf_op jit(solution)/shard_map/pallas_call | solution.py:361
  46.1 13.9 %shard_map.112.before_ref = f32[8,128,2048]{2,1,0:T(8,128)} custom-call(s32[3]{0:T(128)S(1)} %pad_add_fusion.place_ref, f32[8,128,2048]{2,1,0:T(8,128)} %shard_map.111.before_ref, f32[8,24,768]{2,1,0:T(8,128)S(1)} %collective-permute-done.5.fields_ref, bf16[128,48]{1,0:T(8,128)(2,1)S(1)} %bitcast.80, ...), custom_call_target="tpu_custom_call", output_to_operand_aliasing={{}: (1, {})} | custom-call | flops 16000000000 | bytes 4800000 | tf_op jit(solution)/shard_map/pallas_call | solution.py:361
  60.0 0.3 collective-permute-start.7
  60.3 13.9 %shard_map.113.before_ref = f32[8,128,2048]{2,1,0:T(8,128)} custom-call(s32[3]{0:T(128)S(1)} %pad_add_fusion.place_ref, f32[8,128,2048]{2,1,0:T(8,128)} %shard_map.112.before_ref, f32[8,24,768]{2,1,0:T(8,128)S(1)} %collective-permute-done.6.fields_ref, bf16[128,48]{1,0:T(8,128)(2,1)S(1)} %bitcast.81, ...), custom_call_target="tpu_custom_call", output_to_operand_aliasing={{}: (1, {})} | custom-call | flops 16000000000 | bytes 4800000 | tf_op jit(solution)/shard_map/pallas_call | solution.py:361
  74.2 14.0 %shard_map.114 = f32[8,128,2048]{2,1,0:T(8,128)} custom-call(s32[3]{0:T(128)S(1)} %pad_add_fusion.place_ref, f32[8,128,2048]{2,1,0:T(8,128)} %shard_map.113.before_ref, f32[8,24,768]{2,1,0:T(8,128)S(1)} %collective-permute-done.7.fields_ref, bf16[128,48]{1,0:T(8,128)(2,1)S(1)} %bitcast.82, bf16[128,512]{1,0:T(8,128)(2,1)S(1)} %bitcast.72), custom_call_target="tpu_custom_call", output_to_operand_aliasing={{}: (1, {})} | custom-call | flops 16000000000 | bytes 4800000 | tf_op jit(solution)/shard_map/pallas_call | solution.py:361
  88.2 16.2 %shard_map.115 = f32[8,2,64,2048]{3,2,1,0:T(8,128)} custom-call(s32[3]{0:T(128)S(1)} %pad_add_fusion.place_ref, f32[2,2]{1,0:T(2,128)S(1)} %copy-done.3, f32[8,2,64,2048]{3,2,1,0:T(8,128)} %bitcast.87, bf16[2,256,256]{2,1,0:T(8,128)(2,1)S(1)} %copy-done, bf16[2,256,256]{2,1,0:T(8,128)(2,1)S(1)} %copy-done.1, f32[2,16,128]{2,1,0:T(8,128)S(1)} %copy-done.2), custom_call_target="tpu_custom_call" | custom-call | tf_op jit(solution)/shard_map/pallas_call | solution.py:407
  104.4 13.1 %shard_map.116.before_ref = f32[32,2,768]{2,1,0:T(2,128)S(1)} custom-call(s32[3]{0:T(128)S(1)} %pad_add_fusion.place_ref, f32[8,128]{1,0:T(8,128)S(1)} %broadcast_3_before_ref.2.before_ref, f32[8,24,768]{2,1,0:T(8,128)S(1)} %pad_maximum_fusion.fields_ref, f32[8,128,2048]{2,1,0:T(8,128)} %bitcast.88, bf16[128,48]{1,0:T(8,128)(2,1)S(1)} %bitcast.83, ...), custom_call_target="tpu_custom_call" | custom-call | flops 16000000000 | bytes 4800000 | tf_op jit(solution)/shard_map/pallas_call | solution.py:431
  117.6 12.9 %shard_map.117.before_ref = f32[32,2,768]{2,1,0:T(2,128)S(1)} custom-call(s32[3]{0:T(128)S(1)} %pad_add_fusion.place_ref, f32[32,2,768]{2,1,0:T(2,128)S(1)} %shard_map.116.before_ref, f32[8,24,768]{2,1,0:T(8,128)S(1)} %collective-permute-done.5.fields_ref, f32[8,128,2048]{2,1,0:T(8,128)} %bitcast.89, ...), custom_call_target="tpu_custom_call", output_to_operand_aliasing={{}: (1, {})} | custom-call | flops 16000000000 | bytes 4800000 | tf_op jit(solution)/shard_map/pallas_call | solution.py:431
  130.5 12.9 %shard_map.118.before_ref = f32[32,2,768]{2,1,0:T(2,128)S(1)} custom-call(s32[3]{0:T(128)S(1)} %pad_add_fusion.place_ref, f32[32,2,768]{2,1,0:T(2,128)S(1)} %shard_map.117.before_ref, f32[8,24,768]{2,1,0:T(8,128)S(1)} %collective-permute-done.6.fields_ref, f32[8,128,2048]{2,1,0:T(8,128)} %bitcast.90, ...), custom_call_target="tpu_custom_call", output_to_operand_aliasing={{}: (1, {})} | custom-call | flops 16000000000 | bytes 4800000 | tf_op jit(solution)/shard_map/pallas_call | solution.py:431
  143.4 12.9 %shard_map.119 = f32[32,2,768]{2,1,0:T(2,128)S(1)} custom-call(s32[3]{0:T(128)S(1)} %pad_add_fusion.place_ref, f32[32,2,768]{2,1,0:T(2,128)S(1)} %shard_map.118.before_ref, f32[8,24,768]{2,1,0:T(8,128)S(1)} %collective-permute-done.7.fields_ref, f32[8,128,2048]{2,1,0:T(8,128)} %bitcast.91, ...), custom_call_target="tpu_custom_call", output_to_operand_aliasing={{}: (1, {})} | custom-call | flops 16000000000 | bytes 4800000 | tf_op jit(solution)/shard_map/pallas_call | solution.py:431
  156.3 11.7 %all_to_all.5 = f32[32,2,768]{2,1,0:T(2,128)S(1)} all-to-all(f32[32,2,768]{2,1,0:T(2,128)S(1)} %shard_map.119), channel_id=1, replica_groups=mesh['pencil'=8,'depth'=4] {'pencil','depth'}, dimensions={0} | all-to-all | bytes 393216 | tf_op jit(solution)/shard_map/all_to_all | solution.py:458
  168.0 0.6 add.36
  (32 shorter events, 1.1 us)
Async XLA Ops:
  0.0 16.9 %copy-start.4 = (f32[12,2,128,128]{3,2,1,0:T(8,128)S(1)}, f32[12,2,128,128]{3,2,1,0:T(8,128)}, u32[]{:S(2)}) copy-start(f32[12,2,128,128]{3,2,1,0:T(8,128)} %param.16) | copy-start | bytes 4718596
  0.0 13.5 %collective-permute-start.4 = (f32[2,768]{1,0:T(2,128)}, f32[2,768]{1,0:T(2,128)S(1)}, u32[]{:S(2)}, u32[]{:S(2)}) collective-permute-start(f32[2,768]{1,0:T(2,128)} %param.11), channel_id=1, source_target_pairs={{4,0},{8,4},{12,8},{16,12},{20,16},{24,20},{28,24},{5,1},{9,5},{13... | collective-permute-start | bytes 18440 | tf_op jit(solution)/shard_map/ppermute | solution.py:385
  1.4 12.1 %collective-permute-start.3 = (f32[2,768]{1,0:T(2,128)}, f32[2,768]{1,0:T(2,128)S(1)}, u32[]{:S(2)}, u32[]{:S(2)}) collective-permute-start(f32[2,768]{1,0:T(2,128)} %param.11), channel_id=1, source_target_pairs={{0,4},{4,8},{8,12},{12,16},{16,20},{20,24},{24,28},{1,5},{5,9},{9,... | collective-permute-start | bytes 18440 | tf_op jit(solution)/shard_map/ppermute | solution.py:383
  8.4 13.2 %collective-permute-start = (f32[1,24,768]{2,1,0:T(8,128)S(1)}, f32[1,24,768]{2,1,0:T(8,128)S(1)}, u32[]{:S(2)}, u32[]{:S(2)}) collective-permute-start(f32[1,24,768]{2,1,0:T(8,128)S(1)} %bitcast.92), channel_id=1, source_target_pairs={{0,16},{4,20},{8,24},{12,28},{16,0},{20,4},{24,8},{28,12},{1,17},{... | collective-permute-start | bytes 221192 | tf_op jit(solution)/shard_map/ppermute | solution.py:274
  21.6 6.0 %collective-permute-start.1 = (f32[2,24,768]{2,1,0:T(8,128)S(1)}, f32[2,24,768]{2,1,0:T(8,128)S(1)}, u32[]{:S(2)}, u32[]{:S(2)}) collective-permute-start(f32[2,24,768]{2,1,0:T(8,128)S(1)} %pad_maximum_fusion.2.fields_ref), channel_id=1, source_target_pairs={{0,8},{4,12},{8,0},{12,4},{16,24},{20,28},{24,16},{28,20},{1,9},{5... | collective-permute-start | bytes 442376 | tf_op jit(solution)/shard_map/ppermute | solution.py:274
  27.6 6.8 %collective-permute-start.2 = (f32[4,24,768]{2,1,0:T(8,128)S(1)}, f32[4,24,768]{2,1,0:T(8,128)S(1)}, u32[]{:S(2)}, u32[]{:S(2)}) collective-permute-start(f32[4,24,768]{2,1,0:T(8,128)S(1)} %pad_maximum_fusion.1), channel_id=1, source_target_pairs={{0,4},{4,0},{8,12},{12,8},{16,20},{20,16},{24,28},{28,24},{1,5},{5... | collective-permute-start | bytes 884744 | tf_op jit(solution)/shard_map/ppermute | solution.py:274
  34.4 11.6 %collective-permute-start.5 = (f32[8,24,768]{2,1,0:T(8,128)S(1)}, f32[8,24,768]{2,1,0:T(8,128)S(1)}, u32[]{:S(2)}, u32[]{:S(2)}) collective-permute-start(f32[8,24,768]{2,1,0:T(8,128)S(1)} %pad_maximum_fusion.fields_ref), channel_id=1, source_target_pairs={{0,1},{1,0},{2,3},{3,2},{4,5},{5,4},{6,7},{7,6},{8,9},{9,8},{10,11... | collective-permute-start | bytes 1769480 | tf_op jit(solution)/shard_map/ppermute | solution.py:274
  37.2 22.8 %collective-permute-start.6 = (f32[8,24,768]{2,1,0:T(8,128)S(1)}, f32[8,24,768]{2,1,0:T(8,128)S(1)}, u32[]{:S(2)}, u32[]{:S(2)}) collective-permute-start(f32[8,24,768]{2,1,0:T(8,128)S(1)} %pad_maximum_fusion.fields_ref), channel_id=1, source_target_pairs={{0,2},{1,3},{2,0},{3,1},{4,6},{5,7},{6,4},{7,5},{8,10},{9,11},{10,... | collective-permute-start | bytes 1769480 | tf_op jit(solution)/shard_map/ppermute | solution.py:274
  60.0 14.3 %collective-permute-start.7 = (f32[8,24,768]{2,1,0:T(8,128)S(1)}, f32[8,24,768]{2,1,0:T(8,128)S(1)}, u32[]{:S(2)}, u32[]{:S(2)}) collective-permute-start(f32[8,24,768]{2,1,0:T(8,128)S(1)} %collective-permute-done.6.fields_ref), channel_id=1, source_target_pairs={{0,1},{1,0},{2,3},{3,2},{4,5},{5,4},{6,7},{7,6},{8,9},{9,8},{10,11... | collective-permute-start | bytes 1769480 | tf_op jit(solution)/shard_map/ppermute | solution.py:274
  74.2 14.0 %copy-start = (bf16[2,256,256]{2,1,0:T(8,128)(2,1)S(1)}, bf16[2,256,256]{2,1,0:T(8,128)(2,1)}, u32[]{:S(2)}) copy-start(bf16[2,256,256]{2,1,0:T(8,128)(2,1)} %constant.73.clone.forward_ref) | copy-start | bytes 786436
  74.2 14.0 %copy-start.1 = (bf16[2,256,256]{2,1,0:T(8,128)(2,1)S(1)}, bf16[2,256,256]{2,1,0:T(8,128)(2,1)}, u32[]{:S(2)}) copy-start(bf16[2,256,256]{2,1,0:T(8,128)(2,1)} %constant.74.clone.inverse_ref) | copy-start | bytes 786436
  74.2 14.0 %copy-start.2 = (f32[2,16,128]{2,1,0:T(8,128)S(1)}, f32[2,16,128]{2,1,0:T(8,128)}, u32[]{:S(2)}) copy-start(f32[2,16,128]{2,1,0:T(8,128)} %constant.75.clone.twist_ref) | copy-start | bytes 49156
  74.2 14.0 %copy-start.3 = (f32[2,2]{1,0:T(2,128)S(1)}, f32[2,2]{1,0:T(2,128)}, u32[]{:S(2)}) copy-start(f32[2,2]{1,0:T(2,128)} %soil_ref.1) | copy-start | bytes 52
